TPU v7x, 32 devices: a whole 2x2x4 slice. The times are simulated.
32 devices in a mesh: groups: 2 (over y), segment: 4 (over z), inner: 4 (over x, core).
Axes of the slice: x: 2, y: 2, z: 4, core: 2. Of those that a mesh axis runs over, the one named last changes fastest.
Arguments:
- tokens: int32 [3, 64], P(None, 'groups'), parts along dimension 1, may hold values from 0 to 511
- embedding: bfloat16 [512, 4096], P(None, 'inner'), may hold values from -6 to 6
- in_proj: bfloat16 [4, 3, 4096, 4096], P('segment', None, None, 'inner'), may hold values from -0.09375 to 0.09375
- out_proj: bfloat16 [4, 4096, 4096], P('segment', 'inner'), may hold values from -0.09375 to 0.09375
- norm_gain: float32 [4, 4096], P('segment'), may hold values from 0.1 to 1.9
- fir_taps: float32 [4, 7, 4096], P('segment', None, 'inner'), may hold values from -2 to 2
- modal_rate: float32 [4, 8, 4096], P('segment', None, 'inner'), may hold values from 0.05 to 3
- modal_residue: float32 [4, 8, 4096], P('segment', None, 'inner'), may hold values from -2 to 2
- fir_state: float32 [4, 64, 6, 4096], P('segment', 'groups', None, 'inner'), parts along dimension 1, may hold values from -6 to 6
- modal_state: float32 [4, 64, 8, 4096], P('segment', 'groups', None, 'inner'), parts along dimension 1, may hold values from -6 to 6
- final_gain: float32 [4096], replicated, may hold values from 0.1 to 1.9
- unembed: bfloat16 [4096, 512], P(None, 'inner'), may hold values from -0.25 to 0.25
Outputs:
- logits: float32 [2, 64, 512], P(None, ('groups', 'segment'), 'inner'), parts along dimension 1
- logprob: float32 [2, 64], P(None, ('groups', 'segment')), parts along dimension 1
- fir_state_out: float32 [4, 64, 6, 4096], P('segment', 'groups', None, 'inner'), parts along dimension 1
- modal_state_out: float32 [4, 64, 8, 4096], P('segment', 'groups', None, 'inner'), parts along dimension 1
There are 2 independent parts, one for each index of `groups`. A program takes and returns all parts, laid end to end along the dimension named above; an argument that names none is the same for every part. Nothing has to cross between parts.
All inputs are finite; a program needn't handle non-finite values.
Results may differ from a plain program's by a relative error of at most 0.025.
Values may be sent and summed in bfloat16 or wider, within the bound.
A program may use at most 128 MiB of HBM per device.

v0:
```python
import jax
import jax.numpy as jnp
from jax import lax
from jax.sharding import PartitionSpec as P

MICRO = 2


def from_behind(block, axis, distance):
    devices = range(lax.axis_size(axis))
    route = [(i - distance, i) for i in devices if i - distance in devices]
    return lax.ppermute(block, axis, route)


def normed(values, scale_gain):
    mean_square = jnp.mean(values * values, axis=-1, keepdims=True)
    return values * lax.rsqrt(mean_square + 1e-05) * scale_gain


def short_filter(operands):
    product, fir_rows, modal_rows, taps_local, rate_local, residue_local = operands
    window = jnp.concatenate([fir_rows, product[:, None, :]], axis=1)
    filtered = jnp.sum(window * taps_local[::-1][None], axis=1)
    return (filtered, window[:, 1:], modal_rows)


def modal_filter(operands):
    product, fir_rows, modal_rows, taps_local, rate_local, residue_local = operands
    decay_factor = jnp.exp(-rate_local)
    mode_values = decay_factor[None] * modal_rows + (1.0 - decay_factor[None]) * product[:, None, :]
    filtered = jnp.sum(residue_local[None] * mode_values, axis=1) + taps_local[0][None] * product
    return (filtered, fir_rows, mode_values)


def per_device(
    tokens,
    embedding,
    in_proj,
    out_proj,
    norm_gain,
    fir_taps,
    modal_rate,
    modal_residue,
    fir_state,
    modal_state,
    final_gain,
    unembed,
):
    segment_count = lax.axis_size("segment")
    segment_index = lax.axis_index("segment")
    inner_index = lax.axis_index("inner")
    step_count = tokens.shape[0] - 1
    seq_count = tokens.shape[1]
    block_count = MICRO
    row_count = seq_count // block_count
    item_count = step_count * block_count
    tick_count = item_count + segment_count - 1
    local_width = embedding.shape[1]
    w_in = in_proj[0]
    w_out = out_proj[0]
    gain_local = norm_gain[0]
    taps_local = fir_taps[0]
    rate_local = modal_rate[0]
    residue_local = modal_residue[0]
    is_short = segment_index % 2 == 0
    is_last = segment_index == segment_count - 1

    def advance(carry, tick_index):
        previous, fir_all, modal_all, recorded = carry
        item_index = tick_index - segment_index
        is_valid = (item_index >= 0) & (item_index < item_count)
        clipped = jnp.clip(item_index, 0, item_count - 1)
        step_index = clipped // block_count
        row_start = clipped % block_count * row_count
        incoming = from_behind(previous, "segment", 1)
        token_ids = lax.dynamic_slice(tokens, (step_index, row_start), (1, row_count))[0]
        looked_up = jnp.take(embedding, token_ids, axis=0)
        stream_in = jnp.where(segment_index == 0, looked_up, incoming)
        gathered = lax.all_gather(stream_in, "inner", axis=1, tiled=True)
        normalized = normed(gathered.astype(jnp.float32), gain_local).astype(jnp.bfloat16)
        projected = jnp.einsum("bd,jdc->jbc", normalized, w_in, preferred_element_type=jnp.float32)
        product = projected[1] * projected[2]
        fir_rows = lax.dynamic_slice_in_dim(fir_all, row_start, row_count, 0)
        modal_rows = lax.dynamic_slice_in_dim(modal_all, row_start, row_count, 0)
        filtered, fir_next, modal_next = lax.cond(
            is_short,
            short_filter,
            modal_filter,
            (product, fir_rows, modal_rows, taps_local, rate_local, residue_local),
        )
        fir_all = lax.dynamic_update_slice_in_dim(
            fir_all, jnp.where(is_valid, fir_next, fir_rows), row_start, 0
        )
        modal_all = lax.dynamic_update_slice_in_dim(
            modal_all, jnp.where(is_valid, modal_next, modal_rows), row_start, 0
        )
        gated_rows = (projected[0] * filtered).astype(jnp.bfloat16)
        partial_sum = jnp.dot(gated_rows, w_out, preferred_element_type=jnp.float32)
        mixed_sum = lax.psum_scatter(partial_sum, "inner", scatter_dimension=1, tiled=True)
        stream_out = (stream_in.astype(jnp.float32) + mixed_sum).astype(jnp.bfloat16)
        current = lax.dynamic_slice(
            recorded, (step_index, row_start, jnp.int32(0)), (1, row_count, local_width)
        )
        recorded = lax.dynamic_update_slice(
            recorded,
            jnp.where(is_valid & is_last, stream_out[None], current),
            (step_index, row_start, jnp.int32(0)),
        )
        return ((stream_out, fir_all, modal_all, recorded), None)

    initial = (
        jnp.zeros((row_count, local_width), jnp.bfloat16),
        fir_state[0],
        modal_state[0],
        jnp.zeros((step_count, seq_count, local_width), jnp.bfloat16),
    )
    final_carry, unused = lax.scan(advance, initial, jnp.arange(tick_count, dtype=jnp.int32))
    last_out, fir_final, modal_final, recorded = final_carry
    final_stream = lax.all_gather(recorded, "inner", axis=2, tiled=True)
    head_in = normed(final_stream.astype(jnp.float32), final_gain).astype(jnp.bfloat16)
    logits = jnp.einsum("tsd,dv->tsv", head_in, unembed, preferred_element_type=jnp.float32)
    vocab_local = unembed.shape[1]
    columns = inner_index * vocab_local + jnp.arange(vocab_local, dtype=jnp.int32)
    targets = tokens[1:]
    exp_local = jnp.sum(jnp.exp(logits), axis=-1)
    target_part = jnp.sum(
        jnp.where(columns[None, None, :] == targets[:, :, None], logits, 0.0), axis=-1
    )
    exp_total, target_logit = lax.psum((exp_local, target_part), "inner")
    logprob = target_logit - jnp.log(exp_total)
    logits_kept = jnp.where(is_last, logits, 0.0)
    logprob_kept = jnp.where(is_last, logprob, 0.0)
    logits_out, logprob_out = (
        lax.psum_scatter(logits_kept, "segment", scatter_dimension=1, tiled=True),
        lax.psum_scatter(logprob_kept, "segment", scatter_dimension=1, tiled=True),
    )
    return (logits_out, logprob_out, fir_final[None], modal_final[None])


def solution(mesh):
    return jax.shard_map(
        per_device,
        mesh=mesh,
        in_specs=(
            P(None, "groups"),
            P(None, "inner"),
            P("segment", None, None, "inner"),
            P("segment", "inner", None),
            P("segment", None),
            P("segment", None, "inner"),
            P("segment", None, "inner"),
            P("segment", None, "inner"),
            P("segment", "groups", None, "inner"),
            P("segment", "groups", None, "inner"),
            P(),
            P(None, "inner"),
        ),
        out_specs=(
            P(None, ("groups", "segment"), "inner"),
            P(None, ("groups", "segment")),
            P("segment", "groups", None, "inner"),
            P("segment", "groups", None, "inner"),
        ),
        check_vma=False,
    )
```

profile of v0, /device:TPU:0, one launch (start us, length us, event | category | flops | bytes accessed | tf_op | source)
XLA Modules:
  0.0 421.7 jit_solution(7223854443020577943)
XLA Ops:
  14.5 369.1 %while.19 = (s32[]{:T(128)}, bf16[16,1024]{1,0:T(8,128)(2,1)S(1)}, f32[32,6,1024]{2,1,0:T(8,128)}, f32[32,8,1024]{2,1,0:T(8,128)}, bf16[2,32,1024]{2,1,0:T(8,128...) while((s32[]{:T(128)}, bf16[16,1024]{1,0:T(8,128)(2,1)S(1)}, ...), condition=%wide.region_7.8_spmd.clone, body=%wide.region_0.7_spmd.clone.sunk | while | flops 538412224 | bytes 43820432 | solution.py:117
  26.6 5.4 %all_gather.12 = bf16[16,4096]{1,0:T(8,128)(2,1)S(1)} all-gather(bf16[16,1024]{1,0:T(8,128)(2,1)S(1)} %select_select_fusion.2), channel_id=1, replica_groups=mesh['groups'=2,'segment'=4,'inner'=4] {'inner'}, dimensions={1}, use_global_device_ids=true | all-gather | bytes 163840 | tf_op jit(solution)/shard_map/while/body/eval_jaxpr/all_gather | solution.py:79
  32.1 10.0 %convolution_bitcast_fusion.2 = f32[3,16,1024]{2,1,0:T(8,128)S(1)} fusion(bf16[3,4096,1024]{2,1,0:T(8,128)(2,1)} %get-tuple-element.555, bf16[16,4096]{1,0:T(8,128)(2,1)S(1)} %all_gather.12, f32[4096]{0:T(1024)} %bitcast.78, f32[16]{0:T(128)S(1)} %add_rsqrt_fusion.3), kind=kOutput, calls=%fused_computation.11.clone.1 | convolution fusion | flops 402915328 | bytes 25509952 | tf_op jit(solution)/shard_map/while/body/eval_jaxpr/bd,jdc->jbc/dot_general | solution.py:81
  52.0 16.7 %reduce-scatter.6.cloned.1.call-done = f32[16,1024]{1,0:T(8,128)} async-done(((f32[16,4096]{1,0:T(8,128)}), f32[16,1024]{1,0:T(8,128)}) %reduce-scatter.6.cloned.1.call-update) | async-done | bytes 65552 | tf_op jit(solution)/shard_map/while/body/eval_jaxpr/reduce_scatter | solution.py:99
  80.1 5.4 %all_gather.12 = bf16[16,4096]{1,0:T(8,128)(2,1)S(1)} all-gather(bf16[16,1024]{1,0:T(8,128)(2,1)S(1)} %select_select_fusion.2), channel_id=1, replica_groups=mesh['groups'=2,'segment'=4,'inner'=4] {'inner'}, dimensions={1}, use_global_device_ids=true | all-gather | bytes 163840 | tf_op jit(solution)/shard_map/while/body/eval_jaxpr/all_gather | solution.py:79
  85.6 10.0 %convolution_bitcast_fusion.2 = f32[3,16,1024]{2,1,0:T(8,128)S(1)} fusion(bf16[3,4096,1024]{2,1,0:T(8,128)(2,1)} %get-tuple-element.555, bf16[16,4096]{1,0:T(8,128)(2,1)S(1)} %all_gather.12, f32[4096]{0:T(1024)} %bitcast.78, f32[16]{0:T(128)S(1)} %add_rsqrt_fusion.3), kind=kOutput, calls=%fused_computation.11.clone.1 | convolution fusion | flops 402915328 | bytes 25509952 | tf_op jit(solution)/shard_map/while/body/eval_jaxpr/bd,jdc->jbc/dot_general | solution.py:81
  105.5 15.5 %reduce-scatter.6.cloned.1.call-done = f32[16,1024]{1,0:T(8,128)} async-done(((f32[16,4096]{1,0:T(8,128)}), f32[16,1024]{1,0:T(8,128)}) %reduce-scatter.6.cloned.1.call-update) | async-done | bytes 65552 | tf_op jit(solution)/shard_map/while/body/eval_jaxpr/reduce_scatter | solution.py:99
  132.4 5.4 %all_gather.12 = bf16[16,4096]{1,0:T(8,128)(2,1)S(1)} all-gather(bf16[16,1024]{1,0:T(8,128)(2,1)S(1)} %select_select_fusion.2), channel_id=1, replica_groups=mesh['groups'=2,'segment'=4,'inner'=4] {'inner'}, dimensions={1}, use_global_device_ids=true | all-gather | bytes 163840 | tf_op jit(solution)/shard_map/while/body/eval_jaxpr/all_gather | solution.py:79
  138.0 10.0 %convolution_bitcast_fusion.2 = f32[3,16,1024]{2,1,0:T(8,128)S(1)} fusion(bf16[3,4096,1024]{2,1,0:T(8,128)(2,1)} %get-tuple-element.555, bf16[16,4096]{1,0:T(8,128)(2,1)S(1)} %all_gather.12, f32[4096]{0:T(1024)} %bitcast.78, f32[16]{0:T(128)S(1)} %add_rsqrt_fusion.3), kind=kOutput, calls=%fused_computation.11.clone.1 | convolution fusion | flops 402915328 | bytes 25509952 | tf_op jit(solution)/shard_map/while/body/eval_jaxpr/bd,jdc->jbc/dot_general | solution.py:81
  157.8 15.5 %reduce-scatter.6.cloned.1.call-done = f32[16,1024]{1,0:T(8,128)} async-done(((f32[16,4096]{1,0:T(8,128)}), f32[16,1024]{1,0:T(8,128)}) %reduce-scatter.6.cloned.1.call-update) | async-done | bytes 65552 | tf_op jit(solution)/shard_map/while/body/eval_jaxpr/reduce_scatter | solution.py:99
  184.7 5.4 %all_gather.12 = bf16[16,4096]{1,0:T(8,128)(2,1)S(1)} all-gather(bf16[16,1024]{1,0:T(8,128)(2,1)S(1)} %select_select_fusion.2), channel_id=1, replica_groups=mesh['groups'=2,'segment'=4,'inner'=4] {'inner'}, dimensions={1}, use_global_device_ids=true | all-gather | bytes 163840 | tf_op jit(solution)/shard_map/while/body/eval_jaxpr/all_gather | solution.py:79
  190.3 10.0 %convolution_bitcast_fusion.2 = f32[3,16,1024]{2,1,0:T(8,128)S(1)} fusion(bf16[3,4096,1024]{2,1,0:T(8,128)(2,1)} %get-tuple-element.555, bf16[16,4096]{1,0:T(8,128)(2,1)S(1)} %all_gather.12, f32[4096]{0:T(1024)} %bitcast.78, f32[16]{0:T(128)S(1)} %add_rsqrt_fusion.3), kind=kOutput, calls=%fused_computation.11.clone.1 | convolution fusion | flops 402915328 | bytes 25509952 | tf_op jit(solution)/shard_map/while/body/eval_jaxpr/bd,jdc->jbc/dot_general | solution.py:81
  210.2 15.5 %reduce-scatter.6.cloned.1.call-done = f32[16,1024]{1,0:T(8,128)} async-done(((f32[16,4096]{1,0:T(8,128)}), f32[16,1024]{1,0:T(8,128)}) %reduce-scatter.6.cloned.1.call-update) | async-done | bytes 65552 | tf_op jit(solution)/shard_map/while/body/eval_jaxpr/reduce_scatter | solution.py:99
  237.1 5.4 %all_gather.12 = bf16[16,4096]{1,0:T(8,128)(2,1)S(1)} all-gather(bf16[16,1024]{1,0:T(8,128)(2,1)S(1)} %select_select_fusion.2), channel_id=1, replica_groups=mesh['groups'=2,'segment'=4,'inner'=4] {'inner'}, dimensions={1}, use_global_device_ids=true | all-gather | bytes 163840 | tf_op jit(solution)/shard_map/while/body/eval_jaxpr/all_gather | solution.py:79
  242.6 10.0 %convolution_bitcast_fusion.2 = f32[3,16,1024]{2,1,0:T(8,128)S(1)} fusion(bf16[3,4096,1024]{2,1,0:T(8,128)(2,1)} %get-tuple-element.555, bf16[16,4096]{1,0:T(8,128)(2,1)S(1)} %all_gather.12, f32[4096]{0:T(1024)} %bitcast.78, f32[16]{0:T(128)S(1)} %add_rsqrt_fusion.3), kind=kOutput, calls=%fused_computation.11.clone.1 | convolution fusion | flops 402915328 | bytes 25509952 | tf_op jit(solution)/shard_map/while/body/eval_jaxpr/bd,jdc->jbc/dot_general | solution.py:81
  262.5 15.5 %reduce-scatter.6.cloned.1.call-done = f32[16,1024]{1,0:T(8,128)} async-done(((f32[16,4096]{1,0:T(8,128)}), f32[16,1024]{1,0:T(8,128)}) %reduce-scatter.6.cloned.1.call-update) | async-done | bytes 65552 | tf_op jit(solution)/shard_map/while/body/eval_jaxpr/reduce_scatter | solution.py:99
  289.4 5.4 %all_gather.12 = bf16[16,4096]{1,0:T(8,128)(2,1)S(1)} all-gather(bf16[16,1024]{1,0:T(8,128)(2,1)S(1)} %select_select_fusion.2), channel_id=1, replica_groups=mesh['groups'=2,'segment'=4,'inner'=4] {'inner'}, dimensions={1}, use_global_device_ids=true | all-gather | bytes 163840 | tf_op jit(solution)/shard_map/while/body/eval_jaxpr/all_gather | solution.py:79
  295.0 10.0 %convolution_bitcast_fusion.2 = f32[3,16,1024]{2,1,0:T(8,128)S(1)} fusion(bf16[3,4096,1024]{2,1,0:T(8,128)(2,1)} %get-tuple-element.555, bf16[16,4096]{1,0:T(8,128)(2,1)S(1)} %all_gather.12, f32[4096]{0:T(1024)} %bitcast.78, f32[16]{0:T(128)S(1)} %add_rsqrt_fusion.3), kind=kOutput, calls=%fused_computation.11.clone.1 | convolution fusion | flops 402915328 | bytes 25509952 | tf_op jit(solution)/shard_map/while/body/eval_jaxpr/bd,jdc->jbc/dot_general | solution.py:81
  314.9 15.5 %reduce-scatter.6.cloned.1.call-done = f32[16,1024]{1,0:T(8,128)} async-done(((f32[16,4096]{1,0:T(8,128)}), f32[16,1024]{1,0:T(8,128)}) %reduce-scatter.6.cloned.1.call-update) | async-done | bytes 65552 | tf_op jit(solution)/shard_map/while/body/eval_jaxpr/reduce_scatter | solution.py:99
  347.3 10.0 %convolution_bitcast_fusion.2 = f32[3,16,1024]{2,1,0:T(8,128)S(1)} fusion(bf16[3,4096,1024]{2,1,0:T(8,128)(2,1)} %get-tuple-element.555, bf16[16,4096]{1,0:T(8,128)(2,1)S(1)} %all_gather.12, f32[4096]{0:T(1024)} %bitcast.78, f32[16]{0:T(128)S(1)} %add_rsqrt_fusion.3), kind=kOutput, calls=%fused_computation.11.clone.1 | convolution fusion | flops 402915328 | bytes 25509952 | tf_op jit(solution)/shard_map/while/body/eval_jaxpr/bd,jdc->jbc/dot_general | solution.py:81
  367.2 15.5 %reduce-scatter.6.cloned.1.call-done = f32[16,1024]{1,0:T(8,128)} async-done(((f32[16,4096]{1,0:T(8,128)}), f32[16,1024]{1,0:T(8,128)}) %reduce-scatter.6.cloned.1.call-update) | async-done | bytes 65552 | tf_op jit(solution)/shard_map/while/body/eval_jaxpr/reduce_scatter | solution.py:99
  383.6 6.7 %all_gather.9 = bf16[2,32,4096]{2,1,0:T(8,128)(2,1)S(1)} all-gather(bf16[2,32,1024]{2,1,0:T(8,128)(2,1)S(1)} %get-tuple-element.257), channel_id=1, replica_groups=mesh['groups'=2,'segment'=4,'inner'=4] {'inner'}, dimensions={2}, use_global_device_ids=true | all-gather | bytes 655360 | tf_op jit(solution)/shard_map/all_gather | solution.py:119
  394.1 6.6 %all-reduce.1 = (f32[2,32]{1,0:T(2,128)S(1)}, f32[2,32]{1,0:T(2,128)S(1)}) all-reduce(f32[2,32]{1,0:T(2,128)S(1)} %get-tuple-element.321, f32[2,32]{1,0:T(2,128)S(1)} %get-tuple-element.320), channel_id=1, replica_groups=mesh['groups'=2,'segment'=4,'inner'=4] {'inner'}, use_global_device_ids=true, to_apply=%region_11.12 | all-reduce | flops 128 | bytes 1024 | tf_op jit(solution)/shard_map/psum | solution.py:129
  400.7 11.7 %all-reduce = f32[2,32]{1,0:T(2,128)S(1)} all-reduce(f32[2,32]{1,0:T(2,128)S(1)} %subtract_select_fusion), channel_id=4, replica_groups=mesh['groups'=2,'segment'=4,'inner'=4] {'segment'}, use_global_device_ids=true, to_apply=%region_14.15.clone | all-reduce | flops 64 | bytes 512
  (235 shorter events, 167.9 us)
Async XLA Ops:
  8.0 382.5 %copy-start = (bf16[4096,128]{1,0:T(8,128)(2,1)S(1)}, bf16[4096,128]{1,0:T(8,128)(2,1)}, u32[]{:S(2)}) copy-start(bf16[4096,128]{1,0:T(8,128)(2,1)} %param.27) | copy-start | bytes 3145732
  14.5 376.1 %copy-start.3 = (f32[4096]{0:T(1024)S(1)}, f32[4096]{0:T(1024)}, u32[]{:S(2)}) copy-start(f32[4096]{0:T(1024)} %param.26) | copy-start | bytes 49156
  14.5 397.9 %copy-start.4 = (u32[32]{0:T(128)S(1)}, u32[32]{0:T(128)}, u32[]{:S(2)}) copy-start(u32[32]{0:T(128)} %constant.157) | copy-start | bytes 388
  14.5 54.2 %reduce-scatter.6.cloned.1.call-start = ((), (), s32[]{:S(2)}) async-start(), calls=%async_computation.3 | async-start | bytes 327680 | tf_op jit(solution)/shard_map/while/body/eval_jaxpr/reduce_scatter | solution.py:99
  14.6 11.9 %collective-permute-start = (bf16[16,1024]{1,0:T(8,128)(2,1)S(1)}, bf16[16,1024]{1,0:T(8,128)(2,1)S(1)}, u32[]{:S(2)}, u32[]{:S(2)}) collective-permute-start(bf16[16,1024]{1,0:T(8,128)(2,1)S(1)} %broadcast_select_fusion.3), channel_id=1, source_target_pairs={{0,4},{4,8},{8,12},{1,5},{5,9},{9,13},{2,6},{6,10},{10,14},{3,7},{... | collective-permute-start | bytes 98312 | tf_op jit(solution)/shard_map/while/body/eval_jaxpr/ppermute | solution.py:12
  26.4 15.7 %copy-start.1 = (f32[1,8,1024]{2,1,0:T(8,128)S(1)}, f32[1,8,1024]{2,1,0:T(8,128)}, u32[]{:S(2)}) copy-start(f32[1,8,1024]{2,1,0:T(8,128)} %get-tuple-element.557) | copy-start | bytes 98308 | tf_op jit(solution)/shard_map/while
  69.5 51.4 %reduce-scatter.6.cloned.1.call-start = ((), (), s32[]{:S(2)}) async-start(), calls=%async_computation.3 | async-start | bytes 327680 | tf_op jit(solution)/shard_map/while/body/eval_jaxpr/reduce_scatter | solution.py:99
  69.6 10.4 %collective-permute-start = (bf16[16,1024]{1,0:T(8,128)(2,1)S(1)}, bf16[16,1024]{1,0:T(8,128)(2,1)S(1)}, u32[]{:S(2)}, u32[]{:S(2)}) collective-permute-start(bf16[16,1024]{1,0:T(8,128)(2,1)S(1)} %broadcast_select_fusion.3), channel_id=1, source_target_pairs={{0,4},{4,8},{8,12},{1,5},{5,9},{9,13},{2,6},{6,10},{10,14},{3,7},{... | collective-permute-start | bytes 98312 | tf_op jit(solution)/shard_map/while/body/eval_jaxpr/ppermute | solution.py:12
  79.9 15.7 %copy-start.1 = (f32[1,8,1024]{2,1,0:T(8,128)S(1)}, f32[1,8,1024]{2,1,0:T(8,128)}, u32[]{:S(2)}) copy-start(f32[1,8,1024]{2,1,0:T(8,128)} %get-tuple-element.557) | copy-start | bytes 98308 | tf_op jit(solution)/shard_map/while
  121.9 51.5 %reduce-scatter.6.cloned.1.call-start = ((), (), s32[]{:S(2)}) async-start(), calls=%async_computation.3 | async-start | bytes 327680 | tf_op jit(solution)/shard_map/while/body/eval_jaxpr/reduce_scatter | solution.py:99
  121.9 10.4 %collective-permute-start = (bf16[16,1024]{1,0:T(8,128)(2,1)S(1)}, bf16[16,1024]{1,0:T(8,128)(2,1)S(1)}, u32[]{:S(2)}, u32[]{:S(2)}) collective-permute-start(bf16[16,1024]{1,0:T(8,128)(2,1)S(1)} %broadcast_select_fusion.3), channel_id=1, source_target_pairs={{0,4},{4,8},{8,12},{1,5},{5,9},{9,13},{2,6},{6,10},{10,14},{3,7},{... | collective-permute-start | bytes 98312 | tf_op jit(solution)/shard_map/while/body/eval_jaxpr/ppermute | solution.py:12
  132.3 15.7 %copy-start.1 = (f32[1,8,1024]{2,1,0:T(8,128)S(1)}, f32[1,8,1024]{2,1,0:T(8,128)}, u32[]{:S(2)}) copy-start(f32[1,8,1024]{2,1,0:T(8,128)} %get-tuple-element.557) | copy-start | bytes 98308 | tf_op jit(solution)/shard_map/while
  174.2 51.5 %reduce-scatter.6.cloned.1.call-start = ((), (), s32[]{:S(2)}) async-start(), calls=%async_computation.3 | async-start | bytes 327680 | tf_op jit(solution)/shard_map/while/body/eval_jaxpr/reduce_scatter | solution.py:99
  174.3 10.4 %collective-permute-start = (bf16[16,1024]{1,0:T(8,128)(2,1)S(1)}, bf16[16,1024]{1,0:T(8,128)(2,1)S(1)}, u32[]{:S(2)}, u32[]{:S(2)}) collective-permute-start(bf16[16,1024]{1,0:T(8,128)(2,1)S(1)} %broadcast_select_fusion.3), channel_id=1, source_target_pairs={{0,4},{4,8},{8,12},{1,5},{5,9},{9,13},{2,6},{6,10},{10,14},{3,7},{... | collective-permute-start | bytes 98312 | tf_op jit(solution)/shard_map/while/body/eval_jaxpr/ppermute | solution.py:12
  184.6 15.7 %copy-start.1 = (f32[1,8,1024]{2,1,0:T(8,128)S(1)}, f32[1,8,1024]{2,1,0:T(8,128)}, u32[]{:S(2)}) copy-start(f32[1,8,1024]{2,1,0:T(8,128)} %get-tuple-element.557) | copy-start | bytes 98308 | tf_op jit(solution)/shard_map/while
  226.5 51.5 %reduce-scatter.6.cloned.1.call-start = ((), (), s32[]{:S(2)}) async-start(), calls=%async_computation.3 | async-start | bytes 327680 | tf_op jit(solution)/shard_map/while/body/eval_jaxpr/reduce_scatter | solution.py:99
  226.6 10.4 %collective-permute-start = (bf16[16,1024]{1,0:T(8,128)(2,1)S(1)}, bf16[16,1024]{1,0:T(8,128)(2,1)S(1)}, u32[]{:S(2)}, u32[]{:S(2)}) collective-permute-start(bf16[16,1024]{1,0:T(8,128)(2,1)S(1)} %broadcast_select_fusion.3), channel_id=1, source_target_pairs={{0,4},{4,8},{8,12},{1,5},{5,9},{9,13},{2,6},{6,10},{10,14},{3,7},{... | collective-permute-start | bytes 98312 | tf_op jit(solution)/shard_map/while/body/eval_jaxpr/ppermute | solution.py:12
  236.9 15.7 %copy-start.1 = (f32[1,8,1024]{2,1,0:T(8,128)S(1)}, f32[1,8,1024]{2,1,0:T(8,128)}, u32[]{:S(2)}) copy-start(f32[1,8,1024]{2,1,0:T(8,128)} %get-tuple-element.557) | copy-start | bytes 98308 | tf_op jit(solution)/shard_map/while
  278.9 51.5 %reduce-scatter.6.cloned.1.call-start = ((), (), s32[]{:S(2)}) async-start(), calls=%async_computation.3 | async-start | bytes 327680 | tf_op jit(solution)/shard_map/while/body/eval_jaxpr/reduce_scatter | solution.py:99
  279.0 10.3 %collective-permute-start = (bf16[16,1024]{1,0:T(8,128)(2,1)S(1)}, bf16[16,1024]{1,0:T(8,128)(2,1)S(1)}, u32[]{:S(2)}, u32[]{:S(2)}) collective-permute-start(bf16[16,1024]{1,0:T(8,128)(2,1)S(1)} %broadcast_select_fusion.3), channel_id=1, source_target_pairs={{0,4},{4,8},{8,12},{1,5},{5,9},{9,13},{2,6},{6,10},{10,14},{3,7},{... | collective-permute-start | bytes 98312 | tf_op jit(solution)/shard_map/while/body/eval_jaxpr/ppermute | solution.py:12
  331.2 51.5 %reduce-scatter.6.cloned.1.call-start = ((), (), s32[]{:S(2)}) async-start(), calls=%async_computation.3 | async-start | bytes 327680 | tf_op jit(solution)/shard_map/while/body/eval_jaxpr/reduce_scatter | solution.py:99
  331.3 10.4 %collective-permute-start = (bf16[16,1024]{1,0:T(8,128)(2,1)S(1)}, bf16[16,1024]{1,0:T(8,128)(2,1)S(1)}, u32[]{:S(2)}, u32[]{:S(2)}) collective-permute-start(bf16[16,1024]{1,0:T(8,128)(2,1)S(1)} %broadcast_select_fusion.3), channel_id=1, source_target_pairs={{0,4},{4,8},{8,12},{1,5},{5,9},{9,13},{2,6},{6,10},{10,14},{3,7},{... | collective-permute-start | bytes 98312 | tf_op jit(solution)/shard_map/while/body/eval_jaxpr/ppermute | solution.py:12
  341.6 15.7 %copy-start.1 = (f32[1,8,1024]{2,1,0:T(8,128)S(1)}, f32[1,8,1024]{2,1,0:T(8,128)}, u32[]{:S(2)}) copy-start(f32[1,8,1024]{2,1,0:T(8,128)} %get-tuple-element.557) | copy-start | bytes 98308 | tf_op jit(solution)/shard_map/while
  383.5 30.7 %reduce-scatter.4.cloned.1.call-start = ((), (), s32[]{:S(2)}) async-start(), calls=%async_computation.2 | async-start | bytes 40960 | tf_op jit(solution)/shard_map/reduce_scatter | solution.py:134
  (8 other events, 125.3 us)
Sparse Core Ops, SparseCore 0:
  48.3 20.3 reduce-scatter.5
  101.8 19.1 reduce-scatter.5
  154.1 19.1 reduce-scatter.5
  206.5 19.1 reduce-scatter.5
  258.8 19.1 reduce-scatter.5
  311.1 19.1 reduce-scatter.5
  363.5 19.1 reduce-scatter.5
Sparse Core Ops, SparseCore 1:
  391.6 19.3 reduce-scatter.3
where the time goes:
time: 425 us; the launch traced here: 422 us
  waiting for transfers between devices  110 us (26%)
  matrix products  108 us (25%)
  blocking collectives  62.8 us (15%)
  other arithmetic  48.1 us (11%)
  local copies, waits for them, and re-layouts  45.5 us (11%)
  starting transfers between devices  25.6 us (6%)
  between operations  16.2 us (4%)
  loops' own time  6.16 us (1%)
    reduce_scatter x7, waiting for transfers between devices, advance(): lax.psum_scatter(partial_sum, 'inner', scatter_dimension=1, tiled=True)  110 us
    dot_general x7, matrix products, advance(): jnp.einsum('bd,jdc->jbc', normalized, w_in, preferred_element_type=jnp.fl...  69.7 us
    all_gather x7, blocking collectives, advance(): gathered = lax.all_gather(stream_in, 'inner', axis=1, tiled=True)  37.9 us
    dot_general x7, matrix products, advance(): partial_sum = jnp.dot(gated_rows, w_out, preferred_element_type=jnp.float32)  37.1 us
    ppermute x7, starting transfers between devices, from_behind(): return lax.ppermute(block, axis, route)  25.2 us
    gather x7, local copies, waits for them, and re-layouts, advance(): looked_up = jnp.take(embedding, token_ids, axis=0)  13.8 us
    dynamic_update_slice x7, other arithmetic, advance(): lax.dynamic_update_slice_in_dim(fir_all, jnp.where(is_valid, fir_next, fi...  13.4 us
    dynamic_update_slice x7, other arithmetic, advance(): lax.dynamic_update_slice_in_dim(modal_all, jnp.where(is_valid, modal_next...  13.2 us
  transfers between devices with their start and end apart: 15, of which 7 were waited for; matrix products, arithmetic and copies ran while one was open for 18% of the time, Pallas kernels for 0%

commit v1 on v0

v1 whole, which is shorter than its diff:
```python
import functools

import jax
import jax.numpy as jnp
from jax import lax
from jax.experimental import pallas as pl
from jax.experimental.pallas import tpu as pltpu
from jax.sharding import PartitionSpec as P

EPS = 1e-05
MESH = pl.DeviceIdType.MESH
F32 = jnp.float32
BF16 = jnp.bfloat16


def column_of(row, first, count):
    length = row.shape[1]
    down = lax.broadcasted_iota(jnp.int32, (count, length), 0) + first
    across = lax.broadcasted_iota(jnp.int32, (count, length), 1)
    picked = jnp.where(down == across, jnp.broadcast_to(row, (count, length)), 0.0)
    return jnp.sum(picked, axis=1, keepdims=True)


def kernel(
    pieces, inner, segments,
    tokens, norm_gain, final_gain, taps, rate, residue,
    embedding, w_in, w_out, fir_state, modal_state, unembed,
    logits_out, logprob_out, product_out,
    emb_v, in_v, out_v, fir_v, modal_v, unembed_v,
    xbuf, fbuf, sbuf, rbuf, zbuf, acc, squares, state_part, gated,
    head_acc, scatter, lbuf, ebuf,
    emb_sem, in_sem, out_sem, state_sem, unembed_sem,
    x_send, x_recv, r_send, r_recv, z_send, f_send, f_recv, l_send, l_recv, e_send, e_recv,
):
    seg = lax.axis_index("segment")
    me = lax.axis_index("inner")
    last = segments - 1
    steps = tokens.shape[0] - 1
    seqs = tokens.shape[1]
    rows = steps * seqs
    width = emb_v.shape[1]
    sub = width // pieces
    vocab = emb_v.shape[0]
    vocab_local = unembed.shape[1]
    block = seqs // segments
    depth = fir_v.shape[1]
    full = inner * width
    is_short = seg % 2 == 0

    def peer(p):
        return (me // 2 + p // 2) % (inner // 2) * 2 + (me + p) % 2

    barrier = pltpu.get_barrier_semaphore()
    for p in range(1, inner):
        pl.semaphore_signal(barrier, inc=1, device_id={"inner": peer(p)}, device_id_type=MESH)
    for d in range(1, segments):
        pl.semaphore_signal(
            barrier, inc=1, device_id={"segment": (seg + d) % segments}, device_id_type=MESH
        )

    def emb_copy():
        return pltpu.make_async_copy(embedding, emb_v, emb_sem)

    def fir_copy():
        return pltpu.make_async_copy(fir_state.at[0], fir_v, state_sem)

    def modal_copy():
        return pltpu.make_async_copy(modal_state.at[0], modal_v, state_sem)

    def in_copy(k, q):
        return pltpu.make_async_copy(
            w_in.at[0, :, pl.ds(pl.multiple_of(q * width + k * sub, sub), sub), :],
            in_v.at[q * pieces + k],
            in_sem.at[q * pieces + k],
        )

    def out_copy(k, q):
        return pltpu.make_async_copy(
            w_out.at[0, :, pl.ds(pl.multiple_of(q * width + k * sub, sub), sub)],
            out_v.at[q * pieces + k],
            out_sem.at[q * pieces + k],
        )

    def unembed_copy():
        return pltpu.make_async_copy(unembed, unembed_v, unembed_sem)

    @pl.when(seg == 0)
    def _():
        emb_copy().start()

    @pl.when(is_short)
    def _():
        fir_copy().start()

    @pl.when(jnp.logical_not(is_short))
    def _():
        modal_copy().start()

    @pl.loop(0, pieces)
    def _(k):
        in_copy(k, me).start()

    @pl.loop(0, pieces * (inner - 1))
    def _(t):
        in_copy(t // (inner - 1), peer(t % (inner - 1) + 1)).start()

    @pl.loop(0, pieces * inner)
    def _(t):
        out_copy(t // inner, peer((t + 1) % inner)).start()

    unembed_copy().start()
    pl.semaphore_wait(barrier, inner - 1 + segments - 1)

    def x_copy(k, p):
        return pltpu.make_async_remote_copy(
            src_ref=xbuf.at[k * inner + me],
            dst_ref=xbuf.at[k * inner + me],
            send_sem=x_send.at[k * inner + p],
            recv_sem=x_recv.at[k * inner + me],
            device_id={"inner": peer(p)},
            device_id_type=MESH,
        )

    def x_arrival(k, q):
        return pltpu.make_async_copy(
            xbuf.at[k * inner + q], xbuf.at[k * inner + q], x_recv.at[k * inner + q]
        )

    def x_forward(k):
        for p in range(inner - 1, 0, -1):
            x_copy(k, p).start()

    @pl.when(seg == 0)
    def _():
        emb_copy().wait()
        for k in range(pieces):
            for t in range(steps):
                ids = column_of(tokens[pl.ds(t, 1), :].astype(F32), 0, seqs)
                ids = ids.astype(jnp.int32)
                hot = lax.broadcasted_iota(jnp.int32, (seqs, vocab), 1) == ids
                hot = hot.astype(F32).astype(BF16)
                looked_up = jnp.dot(
                    hot, emb_v[:, k * sub:(k + 1) * sub], preferred_element_type=F32
                )
                xbuf[k * inner + me, t * seqs:(t + 1) * seqs, :] = looked_up.astype(BF16)
            x_forward(k)

    @pl.when(is_short)
    def _():
        fir_copy().wait()

        @pl.loop(0, seqs)
        def _(b):
            rows_b = fir_v[b]
            for t in range(steps):
                total = jnp.zeros((1, width), F32)
                for i in range(depth - t):
                    total = total + rows_b[i + t:i + t + 1, :] * taps[0, depth - i:depth - i + 1, :]
                state_part[t, pl.ds(b, 1), :] = total

    @pl.when(jnp.logical_not(is_short))
    def _():
        modal_copy().wait()
        decay = jnp.exp(-rate[0])

        @pl.loop(0, seqs)
        def _(b):
            value = modal_v[b]
            for t in range(steps):
                value = value * decay
                state_part[t, pl.ds(b, 1), :] = jnp.sum(value * residue[0], axis=0, keepdims=True)

    acc[...] = jnp.zeros_like(acc)
    squares[...] = jnp.zeros_like(squares)

    def consume(k, q):
        values = xbuf[k * inner + q].astype(F32)
        total = squares[...]
        for c in range(sub // 128):
            piece = values[:, c * 128:(c + 1) * 128]
            total = total + piece * piece
        squares[...] = total
        offset = pl.multiple_of(q * width + k * sub, sub)
        scaled = (values * norm_gain[:, pl.ds(offset, sub)]).astype(BF16)
        in_copy(k, q).wait()
        for j in range(3):
            acc[j] += jnp.dot(scaled, in_v[q * pieces + k, j], preferred_element_type=F32)

    @pl.loop(0, pieces)
    def _(k):
        @pl.when(seg > 0)
        def _():
            x_arrival(k, me).wait()
            x_forward(k)

        consume(k, me)

    @pl.loop(0, pieces * (inner - 1))
    def _(t):
        k = t // (inner - 1)
        q = peer(t % (inner - 1) + 1)
        x_arrival(k, q).wait()
        consume(k, q)

    scale = lax.rsqrt(jnp.sum(squares[...], axis=1, keepdims=True) / full + EPS)

    decay_all = jnp.exp(-rate[0])
    coefs = []
    power = jnp.ones_like(decay_all)
    for m in range(steps):
        modal_coef = jnp.sum(residue[0] * power * (1.0 - decay_all), axis=0, keepdims=True)
        if m == 0:
            modal_coef = modal_coef + taps[0, 0:1, :]
        power = power * decay_all
        short_coef = taps[0, m:m + 1, :] if m <= depth else jnp.zeros((1, width), F32)
        coefs.append(jnp.where(is_short, short_coef, modal_coef))
    for c in range(0, width, sub):
        cols = slice(c, c + sub)
        products = []
        for t in range(steps):
            part = slice(t * seqs, (t + 1) * seqs)
            scale_t = scale[part]
            product = (acc[1, part, cols] * scale_t) * (acc[2, part, cols] * scale_t)
            products.append(product)
            product_out[t, :, cols] = product
            filtered = state_part[t, :, cols]
            for u in range(t + 1):
                filtered = filtered + coefs[t - u][:, cols] * products[u]
            gated[part, cols] = (acc[0, part, cols] * scale_t * filtered).astype(BF16)

    def r_copy(k, p):
        q = peer(p)
        return pltpu.make_async_remote_copy(
            src_ref=sbuf.at[k * inner + q],
            dst_ref=rbuf.at[k * inner + me],
            send_sem=r_send.at[k * inner + p],
            recv_sem=r_recv.at[k * inner + me],
            device_id={"inner": q},
            device_id_type=MESH,
        )

    def r_arrival(k, q):
        return pltpu.make_async_copy(
            rbuf.at[k * inner + q], rbuf.at[k * inner + q], r_recv.at[k * inner + q]
        )

    def z_copy(k):
        return pltpu.make_async_remote_copy(
            src_ref=zbuf.at[k],
            dst_ref=xbuf.at[k * inner + me],
            send_sem=z_send.at[k],
            recv_sem=x_recv.at[k * inner + me],
            device_id={"segment": (seg + 1) % segments},
            device_id_type=MESH,
        )

    def f_copy(k, p):
        return pltpu.make_async_remote_copy(
            src_ref=zbuf.at[k],
            dst_ref=fbuf.at[k * inner + me],
            send_sem=f_send.at[k * inner + p],
            recv_sem=f_recv.at[k * inner + me],
            device_id={"inner": peer(p)},
            device_id_type=MESH,
        )

    def f_arrival(k, q):
        return pltpu.make_async_copy(
            fbuf.at[k * inner + q], fbuf.at[k * inner + q], f_recv.at[k * inner + q]
        )

    @pl.loop(0, pieces)
    def _(k):
        @pl.loop(1, inner)
        def _(p):
            q = peer(inner - p)
            out_copy(k, q).wait()
            sbuf[k * inner + q] = jnp.dot(
                gated[...], out_v[q * pieces + k], preferred_element_type=F32
            ).astype(BF16)
            r_copy(k, inner - p).start()

        out_copy(k, me).wait()
        acc[0, :, pl.ds(pl.multiple_of(k * sub, sub), sub)] = jnp.dot(
            gated[...], out_v[me * pieces + k], preferred_element_type=F32
        )

    @pl.loop(0, pieces)
    def _(k):
        total = acc[0, :, pl.ds(pl.multiple_of(k * sub, sub), sub)]
        for p in range(1, inner):
            q = peer(p)
            r_arrival(k, q).wait()
            total = total + rbuf[k * inner + q].astype(F32)
        zbuf[k] = (total + xbuf[k * inner + me].astype(F32)).astype(BF16)

        @pl.when(seg < last)
        def _():
            z_copy(k).start()

        @pl.when(seg == last)
        def _():
            for p in range(inner - 1, 0, -1):
                f_copy(k, p).start()

    unembed_copy().wait()

    def l_copy(s):
        return pltpu.make_async_remote_copy(
            src_ref=scatter.at[s],
            dst_ref=lbuf,
            send_sem=l_send.at[s],
            recv_sem=l_recv,
            device_id={"segment": s},
            device_id_type=MESH,
        )

    @pl.when(seg == last)
    def _():
        head_acc[...] = jnp.zeros_like(head_acc)
        squares[...] = jnp.zeros_like(squares)

        def take(k, q, chunk):
            values = chunk.astype(F32)
            total = squares[...]
            for c in range(sub // 128):
                piece = values[:, c * 128:(c + 1) * 128]
                total = total + piece * piece
            squares[...] = total
            offset = pl.multiple_of(q * width + k * sub, sub)
            scaled = (values * final_gain[:, pl.ds(offset, sub)]).astype(BF16)
            head_acc[:, :vocab_local] += jnp.dot(
                scaled, unembed_v[pl.ds(offset, sub), :], preferred_element_type=F32
            )

        @pl.loop(0, pieces)
        def _(k):
            take(k, me, zbuf[k])

        @pl.loop(0, pieces * (inner - 1))
        def _(t):
            k = t // (inner - 1)
            q = peer(t % (inner - 1) + 1)
            f_arrival(k, q).wait()
            take(k, q, fbuf[k * inner + q])

        final_scale = lax.rsqrt(jnp.sum(squares[...], axis=1, keepdims=True) / full + EPS)
        logits = head_acc[...] * final_scale
        for s in range(segments):
            for t in range(steps):
                start = t * seqs + s * block
                if s < last:
                    scatter[s, t] = logits[start:start + block]
                else:
                    lbuf[t] = logits[start:start + block]
            if s < last:
                l_copy(s).start()

    @pl.when(seg < last)
    def _():
        pltpu.make_async_copy(lbuf, lbuf, l_recv).wait()

    def e_copy(p):
        return pltpu.make_async_remote_copy(
            src_ref=ebuf.at[me],
            dst_ref=ebuf.at[me],
            send_sem=e_send.at[p],
            recv_sem=e_recv.at[me],
            device_id={"inner": peer(p)},
            device_id_type=MESH,
        )

    columns = lax.broadcasted_iota(jnp.int32, (block, vocab_local), 1) + me * vocab_local
    lanes = lax.broadcasted_iota(jnp.int32, (block, 128), 1)
    for t in range(steps):
        logits_t = lbuf[t, :, :vocab_local]
        logits_out[t] = logits_t
        target = column_of(tokens[pl.ds(t + 1, 1), :].astype(F32), seg * block, block)
        hit = columns == target.astype(jnp.int32)
        exp_sum = jnp.sum(jnp.exp(logits_t), axis=1, keepdims=True)
        target_part = jnp.sum(jnp.where(hit, logits_t, 0.0), axis=1, keepdims=True)
        ebuf[me, t] = jnp.where(lanes == 0, exp_sum, target_part)
    for p in range(inner - 1, 0, -1):
        e_copy(p).start()
    sums = ebuf[me]
    for p in range(1, inner):
        q = peer(p)
        pltpu.make_async_copy(ebuf.at[q], ebuf.at[q], e_recv.at[q]).wait()
        sums = sums + ebuf[q]
    for t in range(steps):
        logprob_out[t] = sums[t, :, 1:2] - jnp.log(sums[t, :, 0:1])

    @pl.loop(0, pieces)
    def _(k):
        for p in range(1, inner):
            x_copy(k, p).wait_send()
            r_copy(k, p).wait_send()

        @pl.when(seg < last)
        def _():
            z_copy(k).wait_send()

        @pl.when(seg == last)
        def _():
            for p in range(1, inner):
                f_copy(k, p).wait_send()

    @pl.when(seg == last)
    def _():
        for s in range(segments - 1):
            l_copy(s).wait_send()

    for p in range(1, inner):
        e_copy(p).wait_send()


def per_device(
    inner, segments, tokens, embedding, in_proj, out_proj, norm_gain, fir_taps, modal_rate,
    modal_residue, fir_state, modal_state, final_gain, unembed,
):
    steps = tokens.shape[0] - 1
    seqs = tokens.shape[1]
    rows = steps * seqs
    vocab, width = embedding.shape
    pieces = max(1, width // 256)
    sub = width // pieces
    full = inner * width
    vocab_local = unembed.shape[1]
    padded = max(128, vocab_local)
    block = seqs // segments
    whole = pl.BlockSpec(memory_space=pltpu.VMEM)
    anywhere = pl.BlockSpec(memory_space=pl.ANY)
    dma = pltpu.SemaphoreType.DMA
    logits, logprob, product = pl.pallas_call(
        functools.partial(kernel, pieces, inner, segments),
        out_shape=(
            jax.ShapeDtypeStruct((steps, block, vocab_local), F32),
            jax.ShapeDtypeStruct((steps, block, 1), F32),
            jax.ShapeDtypeStruct((steps, seqs, width), F32),
        ),
        in_specs=[whole] * 6 + [anywhere] * 6,
        out_specs=(whole, whole, whole),
        scratch_shapes=[
            pltpu.VMEM((vocab, width), BF16),
            pltpu.VMEM((inner * pieces, 3, sub, width), BF16),
            pltpu.VMEM((inner * pieces, width, sub), BF16),
            pltpu.VMEM(fir_state.shape[1:], F32),
            pltpu.VMEM(modal_state.shape[1:], F32),
            pltpu.VMEM((full, vocab_local), BF16),
            pltpu.VMEM((pieces * inner, rows, sub), BF16),
            pltpu.VMEM((pieces * inner, rows, sub), BF16),
            pltpu.VMEM((pieces * inner, rows, sub), BF16),
            pltpu.VMEM((pieces * inner, rows, sub), BF16),
            pltpu.VMEM((pieces, rows, sub), BF16),
            pltpu.VMEM((3, rows, width), F32),
            pltpu.VMEM((rows, 128), F32),
            pltpu.VMEM((steps, seqs, width), F32),
            pltpu.VMEM((rows, width), BF16),
            pltpu.VMEM((rows, padded), F32),
            pltpu.VMEM((segments, steps, block, padded), F32),
            pltpu.VMEM((steps, block, padded), F32),
            pltpu.VMEM((inner, steps, block, 128), F32),
            dma,
            dma((inner * pieces,)),
            dma((inner * pieces,)),
            dma,
            dma,
            dma((pieces * inner,)),
            dma((pieces * inner,)),
            dma((pieces * inner,)),
            dma((pieces * inner,)),
            dma((pieces,)),
            dma((pieces * inner,)),
            dma((pieces * inner,)),
            dma((segments,)),
            dma,
            dma((inner,)),
            dma((inner,)),
        ],
        compiler_params=pltpu.CompilerParams(
            collective_id=0, has_side_effects=True, vmem_limit_bytes=52 * 1024 * 1024
        ),
    )(
        tokens, norm_gain, final_gain[None], fir_taps, modal_rate, modal_residue,
        embedding, in_proj, out_proj, fir_state, modal_state, unembed,
    )
    is_short = lax.axis_index("segment") % 2 == 0
    newest = jnp.transpose(product, (1, 0, 2))
    depth = fir_state.shape[2]
    shifted = jnp.concatenate([fir_state[0], newest], axis=1)[:, steps:]
    decay = jnp.exp(-modal_rate[0])[None]
    mode_values = modal_state[0]
    for t in range(steps):
        mode_values = decay * mode_values + (1.0 - decay) * product[t][:, None, :]
    fir_out = jnp.where(is_short, shifted, fir_state[0])
    modal_out = jnp.where(is_short, modal_state[0], mode_values)
    return (logits, logprob[..., 0], fir_out[None], modal_out[None])


def solution(mesh):
    inner = mesh.shape["inner"]
    segments = mesh.shape["segment"]
    return jax.shard_map(
        functools.partial(per_device, inner, segments),
        mesh=mesh,
        in_specs=(
            P(None, "groups"),
            P(None, "inner"),
            P("segment", None, None, "inner"),
            P("segment", "inner", None),
            P("segment", None),
            P("segment", None, "inner"),
            P("segment", None, "inner"),
            P("segment", None, "inner"),
            P("segment", "groups", None, "inner"),
            P("segment", "groups", None, "inner"),
            P(),
            P(None, "inner"),
        ),
        out_specs=(
            P(None, ("groups", "segment"), "inner"),
            P(None, ("groups", "segment")),
            P("segment", "groups", None, "inner"),
            P("segment", "groups", None, "inner"),
        ),
        check_vma=False,
    )
```

time: 425 us -> 97.6 us (0.23)
  waiting for transfers between devices: 110 us -> 0 us
  matrix products: 108 us -> 0 us
  Pallas kernels: 0 us -> 83.9 us
  blocking collectives: 62.8 us -> 0 us
  other arithmetic: 48.1 us -> 3.6 us
  local copies, waits for them, and re-layouts: 45.5 us -> 8.95 us
  starting transfers between devices: 25.6 us -> 0 us
  between operations: 16.2 us -> 0.69 us
  loops' own time: 6.16 us -> 0 us
    reduce_scatter x8 -> x0, waiting for transfers between devices: 110 us -> none  [the longest x7 110 us: advance(): lax.psum_scatter(partial_sum, 'inner', scatter_dimension=1, tiled=True)]
    dot_general x15 -> x0, matrix products: 108 us -> none  [the longest x7 69.7 us: advance(): jnp.einsum('bd,jdc->jbc', normalized, w_in, preferred_element_type=jnp.fl...]
    pallas_call x0 -> x1, Pallas kernels: none -> 83.9 us  [per_device(): pl.pallas_call(functools.partial(kernel, pieces, inner, segments), out_sh...]
    all_gather x8 -> x0, blocking collectives: 44.6 us -> none  [the longest x7 37.9 us: advance(): gathered = lax.all_gather(stream_in, 'inner', axis=1, tiled=True)]
    dynamic_update_slice x21 -> x0, other arithmetic: 32.7 us -> none  [the longest x7 13.4 us: advance(): lax.dynamic_update_slice_in_dim(fir_all, jnp.where(is_valid, fir_next, fi...]
    ppermute x7 -> x0, starting transfers between devices: 25.2 us -> none  [from_behind(): return lax.ppermute(block, axis, route)]
    dynamic_slice x21 -> x0, local copies, waits for them, and re-layouts: 19.2 us -> none  [the longest x7 7.58 us: advance(): fir_rows = lax.dynamic_slice_in_dim(fir_all, row_start, row_count, 0)]
    gather x7 -> x0, local copies, waits for them, and re-layouts: 13.8 us -> none  [advance(): looked_up = jnp.take(embedding, token_ids, axis=0)]
  transfers between devices with their start and end apart: 15 -> 0, of which waited for: 7 -> 0; matrix products, arithmetic and copies ran while one was open for 18% -> 0% of each run, Pallas kernels for 0% -> 0%
where the time goes in v1:
time: 97.6 us; the launch traced here: 97.1 us
  Pallas kernels  83.9 us (86%)
  local copies, waits for them, and re-layouts  8.95 us (9%)
  other arithmetic  3.6 us (4%)
    pallas_call x1, Pallas kernels, per_device(): pl.pallas_call(functools.partial(kernel, pieces, inner, segments), out_sh...  83.9 us
    unnamed x19, local copies, waits for them, and re-layouts  8.93 us

profile of v1, /device:TPU:0, one launch (start us, length us, event | category | flops | bytes accessed | tf_op | source)
XLA Modules:
  0.0 97.1 jit_solution(17685509120602378339)
XLA Ops:
  0.6 0.0 copy-start.6
  0.6 0.0 copy-start.7
  0.7 0.9 copy.18.taps
  1.6 0.8 fusion.2
  2.3 2.6 %copy.19.fir_state = f32[1,32,6,1024]{3,2,1,0:T(8,128)} copy(f32[1,32,6,1024]{3,1,2,0:T(8,128)} %param.20) | data formatting | bytes 1572864 | tf_op args[8]
  4.9 0.0 copy-start
  4.9 1.2 %copy-done = bf16[512,1024]{1,0:T(8,128)(2,1)S(1)} copy-done((bf16[512,1024]{1,0:T(8,128)(2,1)S(1)}, bf16[512,1024]{1,0:T(8,128)(2,1)}, u32[]{:S(2)}) %copy-start) | copy-done | bytes 1048600
  6.1 0.0 copy-start.1
  6.1 0.8 copy-done.1
  6.9 0.0 copy-start.2
  6.9 0.8 copy-done.2
  7.6 0.0 copy-start.3
  7.6 0.7 copy-done.3
  8.4 0.0 copy-start.4
  8.4 0.7 copy-done.4
  9.1 0.0 copy-start.5
  9.1 0.7 copy-done.5
  9.8 83.9 %shard_map.147 = (f32[2,8,128]{2,1,0:T(8,128)S(1)}, f32[2,8,1]{2,1,0:T(8,128)S(1)}, f32[2,32,1024]{2,1,0:T(8,128)S(1)}) custom-call(s32[3,32]{1,0:T(4,128)S(1)} %copy-done.5, f32[1,4096]{1,0:T(1,128)S(1)} %copy-done.3, f32[1,4096]{1,0:T(1,128)S(1)} %bitcast.14, f32[1,7,1024]{2,1,0:T(8,128)S(1)} %copy.18.taps, f32[1,8,1024]{2,1,0:T(8,128)S(1)} %copy-done.1, ...), custom_call_target="tpu_custom_call" | custom-call | tf_op jit(solution)/shard_map/pallas_call | solution.py:434
  93.7 0.6 reduce
  94.3 0.0 copy-done.6
  94.3 1.2 %add_select_fusion = f32[1,32,8,1024]{3,2,1,0:T(8,128)} fusion(f32[1,32,8,1024]{3,2,1,0:T(8,128)S(1)} %copy-done.6, f32[32,1024]{1,0:T(8,128)S(1)} %get-tuple-element.11, f32[32,1024]{1,0:T(8,128)S(1)} %get-tuple-element.10, f32[8,1024]{1,0:T(8,128)S(1)} %get-tuple-element.13, f32[8,1024]{1,0:T(8,128)S(1)} %get-tuple-element.12, pred[]{:T(512)S(6)} %eq.5), kind=kLoop, calls=%fused_computation | loop fusion | flops 1835008 | bytes 2424833 | tf_op jit(solution)/shard_map/jit(_where)/select_n | solution.py:496
  95.6 0.0 copy-done.7
  95.6 1.0 fusion.1
  96.5 0.6 copy.21
  (1 shorter events, 0.0 us)
Async XLA Ops:
  0.6 93.7 %copy-start.6 = (f32[1,32,8,1024]{3,2,1,0:T(8,128)S(1)}, f32[1,32,8,1024]{3,2,1,0:T(8,128)}, u32[]{:S(2)}) copy-start(f32[1,32,8,1024]{3,2,1,0:T(8,128)} %modal_state.1) | copy-start | bytes 3145732
  0.6 94.9 %copy-start.7 = (f32[1,32,6,1024]{3,1,2,0:T(8,128)S(1)}, f32[1,32,6,1024]{3,1,2,0:T(8,128)}, u32[]{:S(2)}) copy-start(f32[1,32,6,1024]{3,1,2,0:T(8,128)} %param.20) | copy-start | bytes 2359300
  4.9 1.2 %copy-start = (bf16[512,1024]{1,0:T(8,128)(2,1)S(1)}, bf16[512,1024]{1,0:T(8,128)(2,1)}, u32[]{:S(2)}) copy-start(bf16[512,1024]{1,0:T(8,128)(2,1)} %embedding.1) | copy-start | bytes 3145732
  6.1 0.8 copy-start.1
  6.9 0.8 copy-start.2
  7.6 0.7 copy-start.3
  8.4 0.7 copy-start.4
  9.1 0.7 copy-start.5

commit v2 on v1

v2 whole, which is shorter than its diff:
```python
import functools

import jax
import jax.numpy as jnp
from jax import lax
from jax.experimental import pallas as pl
from jax.experimental.pallas import tpu as pltpu
from jax.sharding import PartitionSpec as P

EPS = 1e-05
MESH = pl.DeviceIdType.MESH
F32 = jnp.float32
BF16 = jnp.bfloat16


def column_of(row, first, count):
    length = row.shape[1]
    down = lax.broadcasted_iota(jnp.int32, (count, length), 0) + first
    across = lax.broadcasted_iota(jnp.int32, (count, length), 1)
    picked = jnp.where(down == across, jnp.broadcast_to(row, (count, length)), 0.0)
    return jnp.sum(picked, axis=1, keepdims=True)


def kernel(
    pieces, inner, segments,
    tokens_h, norm_gain_h, final_gain_h, taps_h, rate_h, residue_h,
    embedding, w_in, w_out, fir_state, modal_state, unembed,
    packed_out, product_out,
    product_v, tokens, norm_gain, final_gain, taps, rate, residue,
    emb_v, in_v, out_v, fir_v, modal_v, unembed_v,
    xbuf, fbuf, abuf, arbuf, bbuf, brbuf, zbuf, acc, mixed, squares, state_part, coefs, gated,
    head_acc, scatter, lbuf, ebuf,
    product_sem, small_sem, emb_sem, in_sem, out_sem, state_sem, unembed_sem,
    x_send, x_recv, a_send, a_recv, b_send, b_recv, z_send, f_send, f_recv,
    l_send, l_recv, e_send, e_recv,
):
    seg = lax.axis_index("segment")
    me = lax.axis_index("inner")
    last = segments - 1
    chips = inner // 2
    chip = me // 2
    core = me % 2
    steps = tokens.shape[0] - 1
    seqs = tokens.shape[1]
    rows = steps * seqs
    width = emb_v.shape[1]
    sub = width // pieces
    vocab = emb_v.shape[0]
    vocab_local = unembed.shape[1]
    padded = lbuf.shape[2]
    block = seqs // segments
    depth = fir_v.shape[0]
    full = inner * width
    is_short = seg % 2 == 0
    sibling = chip * 2 + (core + 1) % 2

    def member(dx, dc):
        return (chip + dx) % chips * 2 + (core + dc) % 2

    def remote(src, dst, send, recv, where):
        return pltpu.make_async_remote_copy(
            src_ref=src, dst_ref=dst, send_sem=send, recv_sem=recv,
            device_id=where, device_id_type=MESH,
        )

    def arrival(ref, sem):
        pltpu.make_async_copy(ref, ref, sem).wait()

    barrier = pltpu.get_barrier_semaphore()
    for p in range(1, inner):
        pl.semaphore_signal(
            barrier, inc=1, device_id={"inner": member(p // 2, p % 2)}, device_id_type=MESH
        )
    for d in range(1, segments):
        pl.semaphore_signal(
            barrier, inc=1, device_id={"segment": (seg + d) % segments}, device_id_type=MESH
        )

    emb_copy = pltpu.make_async_copy(embedding, emb_v, emb_sem)
    fir_copy = pltpu.make_async_copy(fir_state.at[0], fir_v, state_sem)
    modal_copy = pltpu.make_async_copy(modal_state.at[0], modal_v, state_sem)
    unembed_copy = pltpu.make_async_copy(unembed, unembed_v, unembed_sem)
    small = [
        pltpu.make_async_copy(source, target, small_sem.at[index])
        for index, (source, target) in enumerate((
            (tokens_h, tokens), (taps_h, taps), (rate_h, rate), (residue_h, residue),
            (norm_gain_h, norm_gain), (final_gain_h, final_gain),
        ))
    ]

    def in_copy(q, j):
        return pltpu.make_async_copy(
            w_in.at[0, j, pl.ds(pl.multiple_of(q * width, width), width), :],
            in_v.at[q, j],
            in_sem.at[q * 3 + j],
        )

    def out_copy(q, k):
        return pltpu.make_async_copy(
            w_out.at[0, :, pl.ds(pl.multiple_of(q * width + k * sub, sub), sub)],
            out_v.at[q * pieces + k],
            out_sem.at[q * pieces + k],
        )

    small[0].start()

    @pl.when(seg == 0)
    def _():
        emb_copy.start()

    for copy in small[1:]:
        copy.start()

    @pl.when(is_short)
    def _():
        fir_copy.start()

    @pl.when(jnp.logical_not(is_short))
    def _():
        modal_copy.start()

    @pl.loop(0, inner)
    def _(t):
        q = member(t % chips, t // chips)
        for j in range(3):
            in_copy(q, j).start()

    for dc in (1, 0):
        @pl.loop(0, pieces * chips)
        def _(t):
            out_copy(member(t % chips, dc), t // chips).start()

    unembed_copy.start()
    small[0].wait()

    def gather_copy(buf, source, send, recv, k, dx):
        where = sibling if dx == 0 else member(dx, 0)
        return remote(
            source, buf.at[me * pieces + k], send.at[dx * pieces + k],
            recv.at[me * pieces + k], {"inner": where},
        )

    def hand_on(buf, send, recv, k, dx):
        q = member(dx, 0)
        return remote(
            buf.at[q * pieces + k], buf.at[q * pieces + k],
            send.at[(chips + dx) * pieces + k], recv.at[q * pieces + k], {"inner": sibling},
        )

    def x_copy(k, dx):
        return gather_copy(xbuf, xbuf.at[me * pieces + k], x_send, x_recv, k, dx)

    def f_copy(k, dx):
        return gather_copy(fbuf, zbuf.at[k], f_send, f_recv, k, dx)

    def spread(copy_of, k):
        for dx in range(chips - 1, -1, -1):
            copy_of(k, dx).start()

    def pass_on(buf, send, recv):
        for k in range(pieces):
            for dx in range(1, chips):
                q = member(dx, 0)
                arrival(buf.at[q * pieces + k], recv.at[q * pieces + k])
                hand_on(buf, send, recv, k, dx).start()

    @pl.when(seg == 0)
    def _():
        ids = jnp.concatenate(
            [column_of(tokens[pl.ds(t, 1), :].astype(F32), 0, seqs) for t in range(steps)], axis=0
        ).astype(jnp.int32)
        hot = lax.broadcasted_iota(jnp.int32, (rows, vocab), 1) == ids
        hot = hot.astype(F32).astype(BF16)
        emb_copy.wait()
        for k in range(pieces):
            looked_up = jnp.dot(
                hot, emb_v[:, k * sub:(k + 1) * sub], preferred_element_type=F32
            )
            xbuf[me * pieces + k] = looked_up.astype(BF16)

    pl.semaphore_wait(barrier, inner - 1 + segments - 1)

    @pl.when(seg == 0)
    def _():
        for k in range(pieces):
            spread(x_copy, k)

    for copy in small[1:]:
        copy.wait()

    acc[...] = jnp.zeros_like(acc)
    squares[...] = jnp.zeros_like(squares)

    @pl.when(is_short)
    def _():
        fir_copy.wait()
        for t in range(steps):
            coefs[t] = taps[t] if t <= depth else jnp.zeros((1, width), F32)
            for c in range(0, width, 256):
                cols = slice(c, c + 256)
                total = jnp.zeros((seqs, 256), F32)
                for i in range(depth - t):
                    total = total + fir_v[i + t, :, cols] * taps[depth - i, :, cols]
                state_part[t, :, cols] = total

    @pl.when(jnp.logical_not(is_short))
    def _():
        decay = jnp.exp(-rate[0])
        weight = residue[0] * (1.0 - decay)
        for t in range(steps):
            coef = jnp.sum(weight, axis=0, keepdims=True)
            coefs[t] = coef + taps[0] if t == 0 else coef
            weight = weight * decay
        modal_copy.wait()

        @pl.loop(0, seqs)
        def _(b):
            value = modal_v[b]
            for t in range(steps):
                value = value * decay
                state_part[t, pl.ds(b, 1), :] = jnp.sum(value * residue[0], axis=0, keepdims=True)

    def take(values, gain):
        values = values.astype(F32)
        total = squares[...]
        for c in range(0, width, 128):
            piece = values[:, c:c + 128]
            total = total + piece * piece
        squares[...] = total
        return (values * gain).astype(BF16)

    def block_of(buf, q):
        return jnp.concatenate([buf[q * pieces + k] for k in range(pieces)], axis=1)

    @pl.when(seg > 0)
    def _():
        for k in range(pieces):
            arrival(xbuf.at[me * pieces + k], x_recv.at[me * pieces + k])
            spread(x_copy, k)

    @pl.loop(0, inner)
    def _(t):
        q = member(t % chips, t // chips)

        @pl.when(t == 1)
        def _():
            pass_on(xbuf, x_send, x_recv)

        @pl.when(t >= chips)
        def _():
            for k in range(pieces):
                arrival(xbuf.at[q * pieces + k], x_recv.at[q * pieces + k])

        offset = pl.multiple_of(q * width, width)
        scaled = take(block_of(xbuf, q), norm_gain[:, pl.ds(offset, width)])
        for j in range(3):
            in_copy(q, j).wait()
            acc[j] += jnp.dot(scaled, in_v[q, j], preferred_element_type=F32)

    scale = lax.rsqrt(jnp.sum(squares[...], axis=1, keepdims=True) / full + EPS)
    for c in range(0, width, sub):
        cols = slice(c, c + sub)
        products = []
        for t in range(steps):
            part = slice(t * seqs, (t + 1) * seqs)
            scale_t = scale[part]
            product = (acc[1, part, cols] * scale_t) * (acc[2, part, cols] * scale_t)
            products.append(product)
            product_v[t, :, cols] = product
            filtered = state_part[t, :, cols]
            for u in range(t + 1):
                filtered = filtered + coefs[t - u, :, cols] * products[u]
            gated[part, cols] = (acc[0, part, cols] * scale_t * filtered).astype(BF16)

    product_copy = pltpu.make_async_copy(product_v, product_out, product_sem)
    product_copy.start()

    def a_copy(k):
        return remote(abuf.at[k], arbuf.at[k], a_send.at[k], a_recv.at[k], {"inner": sibling})

    def b_copy(k, dx):
        return remote(
            bbuf.at[dx * pieces + k], brbuf.at[chip * pieces + k], b_send.at[dx * pieces + k],
            b_recv.at[chip * pieces + k], {"inner": member(dx, 0)},
        )

    def z_copy(k):
        return remote(
            zbuf.at[k], xbuf.at[me * pieces + k], z_send.at[k],
            x_recv.at[me * pieces + k], {"segment": (seg + 1) % segments},
        )

    def mix(q, k):
        out_copy(q, k).wait()
        return jnp.dot(gated[...], out_v[q * pieces + k], preferred_element_type=F32)

    @pl.loop(0, pieces)
    def _(k):
        @pl.loop(0, chips)
        def _(x):
            abuf[k, x] = mix(x * 2 + (core + 1) % 2, k).astype(BF16)

        a_copy(k).start()

    @pl.loop(0, pieces)
    def _(k):
        for dx in range(chips - 1, -1, -1):
            mixed[dx] = mix(member(dx, 0), k)
        arrival(arbuf.at[k], a_recv.at[k])
        for dx in range(chips - 1, 0, -1):
            total = mixed[dx] + arbuf[k, (chip + dx) % chips].astype(F32)
            bbuf[dx * pieces + k] = total.astype(BF16)
            b_copy(k, dx).start()
        total = mixed[0] + arbuf[k, chip].astype(F32)
        acc[0, :, pl.ds(pl.multiple_of(k * sub, sub), sub)] = (
            total + xbuf[me * pieces + k].astype(F32)
        )

    @pl.loop(0, pieces)
    def _(k):
        total = acc[0, :, pl.ds(pl.multiple_of(k * sub, sub), sub)]
        for dx in range(1, chips):
            source = (chip + dx) % chips * pieces + k
            arrival(brbuf.at[source], b_recv.at[source])
            total = total + brbuf[source].astype(F32)
        zbuf[k] = total.astype(BF16)

        @pl.when(seg < last)
        def _():
            z_copy(k).start()

        @pl.when(seg == last)
        def _():
            spread(f_copy, k)

    unembed_copy.wait()

    def l_copy(s):
        return remote(scatter.at[s], lbuf, l_send.at[s], l_recv, {"segment": s})

    @pl.when(seg == last)
    def _():
        squares[...] = jnp.zeros_like(squares)
        head_acc[...] = jnp.zeros_like(head_acc)

        def head(values, q):
            offset = pl.multiple_of(q * width, width)
            scaled = take(values, final_gain[:, pl.ds(offset, width)])
            head_acc[:, :vocab_local] += jnp.dot(
                scaled, unembed_v[pl.ds(offset, width), :], preferred_element_type=F32
            )

        head(jnp.concatenate([zbuf[k] for k in range(pieces)], axis=1), me)
        pass_on(fbuf, f_send, f_recv)

        @pl.loop(1, inner)
        def _(t):
            q = member(t % chips, t // chips)

            @pl.when(t >= chips)
            def _():
                for k in range(pieces):
                    arrival(fbuf.at[q * pieces + k], f_recv.at[q * pieces + k])

            head(block_of(fbuf, q), q)

        final_scale = lax.rsqrt(jnp.sum(squares[...], axis=1, keepdims=True) / full + EPS)
        logits = head_acc[...] * final_scale
        for s in range(segments):
            for t in range(steps):
                start = t * seqs + s * block
                if s < last:
                    scatter[s, t] = logits[start:start + block]
                else:
                    lbuf[t] = logits[start:start + block]
            if s < last:
                l_copy(s).start()

    @pl.when(seg < last)
    def _():
        arrival(lbuf, l_recv)

    def e_copy(p):
        return remote(
            ebuf.at[me], ebuf.at[me], e_send.at[p], e_recv.at[me],
            {"inner": member(p // 2, p % 2)},
        )

    columns = lax.broadcasted_iota(jnp.int32, (block, vocab_local), 1) + me * vocab_local
    lanes = lax.broadcasted_iota(jnp.int32, (block, 128), 1)
    for t in range(steps):
        logits_t = lbuf[t, :, :vocab_local]
        packed_out[t, :, :vocab_local] = logits_t
        target = column_of(tokens[pl.ds(t + 1, 1), :].astype(F32), seg * block, block)
        hit = columns == target.astype(jnp.int32)
        exp_sum = jnp.sum(jnp.exp(logits_t), axis=1, keepdims=True)
        target_part = jnp.sum(jnp.where(hit, logits_t, 0.0), axis=1, keepdims=True)
        ebuf[me, t] = jnp.where(lanes == 0, exp_sum, target_part)
    for p in range(inner - 1, 0, -1):
        e_copy(p).start()
    sums = ebuf[me]
    for p in range(1, inner):
        q = member(p // 2, p % 2)
        arrival(ebuf.at[q], e_recv.at[q])
        sums = sums + ebuf[q]
    for t in range(steps):
        logprob = sums[t, :, 1:2] - jnp.log(sums[t, :, 0:1])
        packed_out[t, :, padded:] = jnp.broadcast_to(logprob, (block, 128))

    product_copy.wait()

    @pl.loop(0, pieces)
    def _(k):
        a_copy(k).wait_send()
        for dx in range(chips):
            x_copy(k, dx).wait_send()
            if dx > 0:
                hand_on(xbuf, x_send, x_recv, k, dx).wait_send()
                b_copy(k, dx).wait_send()

        @pl.when(seg < last)
        def _():
            z_copy(k).wait_send()

        @pl.when(seg == last)
        def _():
            for dx in range(chips):
                f_copy(k, dx).wait_send()
                if dx > 0:
                    hand_on(fbuf, f_send, f_recv, k, dx).wait_send()

    @pl.when(seg == last)
    def _():
        for s in range(segments - 1):
            l_copy(s).wait_send()

    for p in range(1, inner):
        e_copy(p).wait_send()


def per_device(
    inner, segments, tokens, embedding, in_proj, out_proj, norm_gain, fir_taps, modal_rate,
    modal_residue, fir_state, modal_state, final_gain, unembed,
):
    steps = tokens.shape[0] - 1
    seqs = tokens.shape[1]
    rows = steps * seqs
    vocab, width = embedding.shape
    pieces = max(1, width // 256)
    sub = width // pieces
    chips = inner // 2
    full = inner * width
    vocab_local = unembed.shape[1]
    padded = max(128, vocab_local)
    block = seqs // segments
    whole = pl.BlockSpec(memory_space=pltpu.VMEM)
    in_hbm = pl.BlockSpec(memory_space=pltpu.HBM)
    dma = pltpu.SemaphoreType.DMA
    fir_by_tap = jnp.transpose(fir_state, (0, 2, 1, 3))
    operands = (
        tokens, norm_gain, final_gain[None], jnp.transpose(fir_taps, (1, 0, 2)), modal_rate,
        modal_residue, embedding, in_proj, out_proj, fir_by_tap, modal_state, unembed,
    )
    packed, product = pl.pallas_call(
        functools.partial(kernel, pieces, inner, segments),
        out_shape=(
            jax.ShapeDtypeStruct((steps, block, padded + 128), F32),
            jax.ShapeDtypeStruct((steps, seqs, width), F32),
        ),
        in_specs=[in_hbm] * len(operands),
        out_specs=(whole, in_hbm),
        scratch_shapes=[
            pltpu.VMEM((steps, seqs, width), F32),
            *[pltpu.VMEM(o.shape, o.dtype) for o in operands[:6]],
            pltpu.VMEM((vocab, width), BF16),
            pltpu.VMEM((inner, 3, width, width), BF16),
            pltpu.VMEM((inner * pieces, width, sub), BF16),
            pltpu.VMEM(fir_by_tap.shape[1:], F32),
            pltpu.VMEM(modal_state.shape[1:], F32),
            pltpu.VMEM((full, vocab_local), BF16),
            pltpu.VMEM((inner * pieces, rows, sub), BF16),
            pltpu.VMEM((inner * pieces, rows, sub), BF16),
            pltpu.VMEM((pieces, chips, rows, sub), BF16),
            pltpu.VMEM((pieces, chips, rows, sub), BF16),
            pltpu.VMEM((chips * pieces, rows, sub), BF16),
            pltpu.VMEM((chips * pieces, rows, sub), BF16),
            pltpu.VMEM((pieces, rows, sub), BF16),
            pltpu.VMEM((3, rows, width), F32),
            pltpu.VMEM((chips, rows, sub), F32),
            pltpu.VMEM((rows, 128), F32),
            pltpu.VMEM((steps, seqs, width), F32),
            pltpu.VMEM((steps, 1, width), F32),
            pltpu.VMEM((rows, width), BF16),
            pltpu.VMEM((rows, padded), F32),
            pltpu.VMEM((segments, steps, block, padded), F32),
            pltpu.VMEM((steps, block, padded), F32),
            pltpu.VMEM((inner, steps, block, 128), F32),
            dma,
            dma((6,)),
            dma,
            dma((inner * 3,)),
            dma((inner * pieces,)),
            dma,
            dma,
            dma((inner * pieces,)),
            dma((inner * pieces,)),
            dma((pieces,)),
            dma((pieces,)),
            dma((chips * pieces,)),
            dma((chips * pieces,)),
            dma((pieces,)),
            dma((inner * pieces,)),
            dma((inner * pieces,)),
            dma((segments,)),
            dma,
            dma((inner,)),
            dma((inner,)),
        ],
        compiler_params=pltpu.CompilerParams(
            collective_id=0, has_side_effects=True, vmem_limit_bytes=60 * 1024 * 1024
        ),
    )(*operands)
    is_short = lax.axis_index("segment") % 2 == 0
    shifted = jnp.concatenate([fir_by_tap[0], product], axis=0)[steps:]
    fir_out = jnp.where(is_short, shifted, fir_by_tap[0])
    decay = jnp.exp(-modal_rate[0])[None]
    mode_values = modal_state[0]
    for t in range(steps):
        mode_values = decay * mode_values + (1.0 - decay) * product[t][:, None, :]
    modal_out = jnp.where(is_short, modal_state[0], mode_values)
    return (
        packed[..., :vocab_local],
        packed[..., padded],
        jnp.transpose(fir_out, (1, 0, 2))[None],
        modal_out[None],
    )


def solution(mesh):
    inner = mesh.shape["inner"]
    segments = mesh.shape["segment"]
    return jax.shard_map(
        functools.partial(per_device, inner, segments),
        mesh=mesh,
        in_specs=(
            P(None, "groups"),
            P(None, "inner"),
            P("segment", None, None, "inner"),
            P("segment", "inner", None),
            P("segment", None),
            P("segment", None, "inner"),
            P("segment", None, "inner"),
            P("segment", None, "inner"),
            P("segment", "groups", None, "inner"),
            P("segment", "groups", None, "inner"),
            P(),
            P(None, "inner"),
        ),
        out_specs=(
            P(None, ("groups", "segment"), "inner"),
            P(None, ("groups", "segment")),
            P("segment", "groups", None, "inner"),
            P("segment", "groups", None, "inner"),
        ),
        check_vma=False,
    )
```

time: 97.6 us -> 93.7 us (0.960)
  local copies, waits for them, and re-layouts: 8.95 us -> 3.64 us
  Pallas kernels: 83.9 us -> 86 us
    unnamed x19 -> x6, local copies, waits for them, and re-layouts: 8.93 us -> 0.01 us
    slice x0 -> x2, local copies, waits for them, and re-layouts: none -> 2.64 us  [the longest x1 1.34 us: per_device(): packed[..., padded]]
    pallas_call x1, Pallas kernels: 83.9 us -> 86 us  [per_device(): pl.pallas_call(functools.partial(kernel, pieces, inner, segments), out_sh...]
where the time goes in v2:
time: 93.7 us; the launch traced here: 93.5 us
  Pallas kernels  86 us (92%)
  local copies, waits for them, and re-layouts  3.64 us (4%)
  other arithmetic  3.13 us (3%)
    pallas_call x1, Pallas kernels, per_device(): pl.pallas_call(functools.partial(kernel, pieces, inner, segments), out_sh...  86 us
    broadcast_in_dim x1, other arithmetic, per_device(): jnp.transpose(fir_out, (1, 0, 2))[None]  1.9 us

profile of v2, /device:TPU:0, one launch (start us, length us, event | category | flops | bytes accessed | tf_op | source)
XLA Modules:
  0.0 93.5 jit_solution(181936777074563305)
XLA Ops:
  0.6 0.0 copy-start.1
  0.6 0.0 copy-start.2
  0.7 0.0 copy-start
  0.7 86.0 %shard_map.147 = (f32[2,8,256]{2,1,0:T(8,128)}, f32[2,32,1024]{2,1,0:T(8,128)}) custom-call(s32[3,32]{1,0:T(4,128)} %tokens_h.1, f32[1,4096]{1,0:T(1,128)} %norm_gain_h.1, f32[1,4096]{1,0:T(1,128)} %bitcast.20, f32[7,1,1024]{2,1,0:T(1,128)} %bitcast.19, f32[1,8,1024]{2,1,0:T(8,128)} %rate_h.1, f32[1,8,1024]{2,1,0:T(8,128)} %residue_h.1, ...), custom_call_target="tpu_custom_call" | custom-call | tf_op jit(solution)/shard_map/pallas_call | solution.py:464
  86.7 1.0 %slice_bitcast_fusion.1 = (f32[32,1024]{1,0:T(8,128)S(1)}, f32[32,1024]{1,0:T(8,128)S(1)}) fusion(f32[2,32,1024]{2,1,0:T(8,128)} %get-tuple-element.7), kind=kLoop, calls=%fused_computation.5 | loop fusion | bytes 524288 | tf_op jit(solution)/shard_map/mul | solution.py:529
  87.7 0.0 copy-done.2
  87.7 0.0 copy-done
  87.7 1.2 %add_select_fusion = f32[1,32,8,1024]{3,2,1,0:T(8,128)} fusion(f32[1,32,8,1024]{3,2,1,0:T(8,128)S(1)} %copy-done, f32[32,1024]{1,0:T(8,128)S(1)} %get-tuple-element.9, f32[32,1024]{1,0:T(8,128)S(1)} %get-tuple-element.8, f32[8,1024]{1,0:T(8,128)S(1)} %get-tuple-element.11, f32[8,1024]{1,0:T(8,128)S(1)} %get-tuple-element.10, pred[]{:T(512)S(6)} %eq.5), kind=kLoop, calls=%fused_computation | loop fusion | flops 1835008 | bytes 2424833 | tf_op jit(solution)/shard_map/jit(_where)/select_n | solution.py:530
  89.0 0.0 copy-done.1
  89.0 1.9 %fusion.1 = f32[1,32,6,1024]{3,1,2,0:T(8,128)} fusion(f32[6,32,1024]{2,1,0:T(8,128)S(1)} %bitcast.18, f32[2,32,1024]{2,1,0:T(8,128)} %get-tuple-element.7, pred[]{:T(512)S(6)} %eq.5), kind=kLoop, calls=%fused_computation.3 | loop fusion | flops 393216 | bytes 1835009 | tf_op jit(solution)/shard_map/broadcast_in_dim | solution.py:534
  90.9 1.3 %slice.15 = f32[2,8,128]{2,1,0:T(8,128)} slice(f32[2,8,256]{2,1,0:T(8,128)} %get-tuple-element.6), slice={[0:2], [0:8], [0:128]} | slice | bytes 16384 | tf_op jit(solution)/shard_map/slice | solution.py:532
  92.2 1.3 %slice_reduce_fusion = f32[2,8]{1,0:T(2,128)} fusion(f32[2,8,256]{2,1,0:T(8,128)} %get-tuple-element.6), kind=kLoop, calls=%fused_computation.9 | loop fusion | bytes 128 | tf_op jit(solution)/shard_map/slice | solution.py:533
  (1 shorter events, 0.0 us)
Async XLA Ops:
  0.6 88.3 %copy-start.1 = (f32[1,32,6,1024]{3,1,2,0:T(8,128)S(1)}, f32[1,32,6,1024]{3,1,2,0:T(8,128)}, u32[]{:S(2)}) copy-start(f32[1,32,6,1024]{3,1,2,0:T(8,128)} %param.20) | copy-start | bytes 2359300
  0.6 87.0 %copy-start.2 = (f32[1,8,1024]{2,1,0:T(8,128)S(1)}, f32[1,8,1024]{2,1,0:T(8,128)}, u32[]{:S(2)}) copy-start(f32[1,8,1024]{2,1,0:T(8,128)} %rate_h.1) | copy-start | bytes 98308
  0.7 87.1 %copy-start = (f32[1,32,8,1024]{3,2,1,0:T(8,128)S(1)}, f32[1,32,8,1024]{3,2,1,0:T(8,128)}, u32[]{:S(2)}) copy-start(f32[1,32,8,1024]{3,2,1,0:T(8,128)} %modal_state.1) | copy-start | bytes 3145732

commit v3 on v2

--- a/solution.py
+++ b/solution.py
@@ -25,12 +25,12 @@
     pieces, inner, segments,
     tokens_h, norm_gain_h, final_gain_h, taps_h, rate_h, residue_h,
     embedding, w_in, w_out, fir_state, modal_state, unembed,
-    packed_out, product_out,
+    packed_out, fir_new, modal_new,
     product_v, tokens, norm_gain, final_gain, taps, rate, residue,
     emb_v, in_v, out_v, fir_v, modal_v, unembed_v,
     xbuf, fbuf, abuf, arbuf, bbuf, brbuf, zbuf, acc, mixed, squares, state_part, coefs, gated,
     head_acc, scatter, lbuf, ebuf,
-    product_sem, small_sem, emb_sem, in_sem, out_sem, state_sem, unembed_sem,
+    out_state_sem, small_sem, emb_sem, in_sem, out_sem, state_sem, unembed_sem,
     x_send, x_recv, a_send, a_recv, b_send, b_recv, z_send, f_send, f_recv,
     l_send, l_recv, e_send, e_recv,
 ):
@@ -119,18 +119,39 @@
     def _():
         modal_copy.start()
 
-    @pl.loop(0, inner)
+    for dx, dc in (
+        [(0, 0), (0, 1)] + [(dx, 0) for dx in range(1, chips)] + [(dx, 1) for dx in range(1, chips)]
+    ):
+        for j in range(3):
+            in_copy(member(dx, dc), j).start()
+
+    @pl.loop(0, pieces * inner)
     def _(t):
-        q = member(t % chips, t // chips)
-        for j in range(3):
-            in_copy(q, j).start()
-
-    for dc in (1, 0):
-        @pl.loop(0, pieces * chips)
-        def _(t):
-            out_copy(member(t % chips, dc), t // chips).start()
+        out_copy(member(t % chips, (t // chips + 1) % 2), t // inner).start()
 
     unembed_copy.start()
+
+    fir_whole = pltpu.make_async_copy(fir_state.at[0], fir_new, out_state_sem.at[0])
+    fir_shift = pltpu.make_async_copy(
+        fir_state.at[0, pl.ds(steps, depth - steps)],
+        fir_new.at[pl.ds(0, depth - steps)],
+        out_state_sem.at[0],
+    )
+    fir_latest = pltpu.make_async_copy(
+        product_v, fir_new.at[pl.ds(depth - steps, steps)], out_state_sem.at[1]
+    )
+    modal_whole = pltpu.make_async_copy(modal_state.at[0], modal_new, out_state_sem.at[2])
+    modal_done = pltpu.make_async_copy(modal_v, modal_new, out_state_sem.at[2])
+
+    @pl.when(is_short)
+    def _():
+        fir_shift.start()
+        modal_whole.start()
+
+    @pl.when(jnp.logical_not(is_short))
+    def _():
+        fir_whole.start()
+
     small[0].wait()
 
     def gather_copy(buf, source, send, recv, k, dx):
@@ -223,7 +244,7 @@
     def take(values, gain):
         values = values.astype(F32)
         total = squares[...]
-        for c in range(0, width, 128):
+        for c in range(0, values.shape[1], 128):
             piece = values[:, c:c + 128]
             total = total + piece * piece
         squares[...] = total
@@ -232,21 +253,34 @@
     def block_of(buf, q):
         return jnp.concatenate([buf[q * pieces + k] for k in range(pieces)], axis=1)
 
-    @pl.when(seg > 0)
-    def _():
-        for k in range(pieces):
+    @pl.loop(0, pieces)
+    def _(k):
+        @pl.when(seg > 0)
+        def _():
             arrival(xbuf.at[me * pieces + k], x_recv.at[me * pieces + k])
             spread(x_copy, k)
 
-    @pl.loop(0, inner)
+        @pl.when(k == 0)
+        def _():
+            for j in range(3):
+                in_copy(me, j).wait()
+
+        offset = pl.multiple_of(me * width + k * sub, sub)
+        scaled = take(xbuf[me * pieces + k], norm_gain[:, pl.ds(offset, sub)])
+        depth_rows = pl.ds(pl.multiple_of(k * sub, sub), sub)
+        for j in range(3):
+            acc[j] += jnp.dot(scaled, in_v[me, j, depth_rows, :], preferred_element_type=F32)
+
+    @pl.loop(1, inner)
     def _(t):
-        q = member(t % chips, t // chips)
-
-        @pl.when(t == 1)
+        q = member(jnp.where(t == 1, 0, jnp.where(t <= chips, t - 1, t - chips)),
+                   jnp.where((t == 1) | (t > chips), 1, 0))
+
+        @pl.when(t == 2)
         def _():
             pass_on(xbuf, x_send, x_recv)
 
-        @pl.when(t >= chips)
+        @pl.when((t == 1) | (t > chips))
         def _():
             for k in range(pieces):
                 arrival(xbuf.at[q * pieces + k], x_recv.at[q * pieces + k])
@@ -272,8 +306,9 @@
                 filtered = filtered + coefs[t - u, :, cols] * products[u]
             gated[part, cols] = (acc[0, part, cols] * scale_t * filtered).astype(BF16)
 
-    product_copy = pltpu.make_async_copy(product_v, product_out, product_sem)
-    product_copy.start()
+    @pl.when(is_short)
+    def _():
+        fir_latest.start()
 
     def a_copy(k):
         return remote(abuf.at[k], arbuf.at[k], a_send.at[k], a_recv.at[k], {"inner": sibling})
@@ -294,44 +329,54 @@
         out_copy(q, k).wait()
         return jnp.dot(gated[...], out_v[q * pieces + k], preferred_element_type=F32)
 
-    @pl.loop(0, pieces)
-    def _(k):
-        @pl.loop(0, chips)
-        def _(x):
-            abuf[k, x] = mix(x * 2 + (core + 1) % 2, k).astype(BF16)
-
-        a_copy(k).start()
-
-    @pl.loop(0, pieces)
-    def _(k):
-        for dx in range(chips - 1, -1, -1):
-            mixed[dx] = mix(member(dx, 0), k)
-        arrival(arbuf.at[k], a_recv.at[k])
-        for dx in range(chips - 1, 0, -1):
-            total = mixed[dx] + arbuf[k, (chip + dx) % chips].astype(F32)
-            bbuf[dx * pieces + k] = total.astype(BF16)
-            b_copy(k, dx).start()
-        total = mixed[0] + arbuf[k, chip].astype(F32)
-        acc[0, :, pl.ds(pl.multiple_of(k * sub, sub), sub)] = (
-            total + xbuf[me * pieces + k].astype(F32)
-        )
-
-    @pl.loop(0, pieces)
-    def _(k):
-        total = acc[0, :, pl.ds(pl.multiple_of(k * sub, sub), sub)]
-        for dx in range(1, chips):
-            source = (chip + dx) % chips * pieces + k
-            arrival(brbuf.at[source], b_recv.at[source])
-            total = total + brbuf[source].astype(F32)
-        zbuf[k] = total.astype(BF16)
-
-        @pl.when(seg < last)
-        def _():
-            z_copy(k).start()
-
-        @pl.when(seg == last)
-        def _():
-            spread(f_copy, k)
+    for step in range(pieces + 2):
+        k = step
+        if k < pieces:
+            for x in range(chips):
+                abuf[k, x] = mix(x * 2 + (core + 1) % 2, k).astype(BF16)
+            a_copy(k).start()
+        k = step - 1
+        if 0 <= k < pieces:
+            arrival(arbuf.at[k], a_recv.at[k])
+            for dx in range(chips - 1, 0, -1):
+                total = mixed[k, dx] + arbuf[k, (chip + dx) % chips].astype(F32)
+                bbuf[dx * pieces + k] = total.astype(BF16)
+                b_copy(k, dx).start()
+            total = mixed[k, 0] + arbuf[k, chip].astype(F32)
+            mixed[k, 0] = total + xbuf[me * pieces + k].astype(F32)
+        k = step
+        if k < pieces:
+            for dx in range(chips - 1, -1, -1):
+                mixed[k, dx] = mix(member(dx, 0), k)
+        k = step - 2
+        if 0 <= k < pieces:
+            total = mixed[k, 0]
+            for dx in range(1, chips):
+                source = (chip + dx) % chips * pieces + k
+                arrival(brbuf.at[source], b_recv.at[source])
+                total = total + brbuf[source].astype(F32)
+            zbuf[k] = total.astype(BF16)
+
+            @pl.when(seg < last)
+            def _():
+                z_copy(k).start()
+
+            @pl.when(seg == last)
+            def _():
+                spread(f_copy, k)
+
+    @pl.when(jnp.logical_not(is_short))
+    def _():
+        decay = jnp.exp(-rate[0])
+
+        @pl.loop(0, seqs)
+        def _(b):
+            value = modal_v[b]
+            for t in range(steps):
+                value = decay * value + (1.0 - decay) * product_v[t, pl.ds(b, 1), :]
+            modal_v[b] = value
+
+        modal_done.start()
 
     unembed_copy.wait()
 
@@ -407,7 +452,16 @@
         logprob = sums[t, :, 1:2] - jnp.log(sums[t, :, 0:1])
         packed_out[t, :, padded:] = jnp.broadcast_to(logprob, (block, 128))
 
-    product_copy.wait()
+    @pl.when(is_short)
+    def _():
+        fir_shift.wait()
+        fir_latest.wait()
+        modal_whole.wait()
+
+    @pl.when(jnp.logical_not(is_short))
+    def _():
+        fir_whole.wait()
+        modal_done.wait()
 
     @pl.loop(0, pieces)
     def _(k):
@@ -436,6 +490,26 @@
 
     for p in range(1, inner):
         e_copy(p).wait_send()
+
+
+def hand_out(vocab_local, padded, packed, fir_new, modal_new, logits, logprob, fir, modal, sems):
+    copies = [
+        pltpu.make_async_copy(fir_new, fir.at[0], sems.at[0]),
+        pltpu.make_async_copy(modal_new, modal.at[0], sems.at[1]),
+    ]
+    for copy in copies:
+        copy.start()
+    steps, block = logprob.shape
+    down = lax.broadcasted_iota(jnp.int32, (block, block), 0)
+    across = lax.broadcasted_iota(jnp.int32, (block, block), 1)
+    for t in range(steps):
+        logits[t] = packed[t, :, :vocab_local]
+        spread_out = packed[t, :, padded:padded + block]
+        logprob[t:t + 1, :] = jnp.sum(
+            jnp.where(down == across, spread_out, 0.0), axis=0, keepdims=True
+        )
+    for copy in copies:
+        copy.wait()
 
 
 def per_device(
@@ -461,14 +535,15 @@
         tokens, norm_gain, final_gain[None], jnp.transpose(fir_taps, (1, 0, 2)), modal_rate,
         modal_residue, embedding, in_proj, out_proj, fir_by_tap, modal_state, unembed,
     )
-    packed, product = pl.pallas_call(
+    packed, fir_new, modal_new = pl.pallas_call(
         functools.partial(kernel, pieces, inner, segments),
         out_shape=(
             jax.ShapeDtypeStruct((steps, block, padded + 128), F32),
-            jax.ShapeDtypeStruct((steps, seqs, width), F32),
+            jax.ShapeDtypeStruct(fir_by_tap.shape[1:], F32),
+            jax.ShapeDtypeStruct(modal_state.shape[1:], F32),
         ),
         in_specs=[in_hbm] * len(operands),
-        out_specs=(whole, in_hbm),
+        out_specs=(whole, in_hbm, in_hbm),
         scratch_shapes=[
             pltpu.VMEM((steps, seqs, width), F32),
             *[pltpu.VMEM(o.shape, o.dtype) for o in operands[:6]],
@@ -486,7 +561,7 @@
             pltpu.VMEM((chips * pieces, rows, sub), BF16),
             pltpu.VMEM((pieces, rows, sub), BF16),
             pltpu.VMEM((3, rows, width), F32),
-            pltpu.VMEM((chips, rows, sub), F32),
+            pltpu.VMEM((pieces, chips, rows, sub), F32),
             pltpu.VMEM((rows, 128), F32),
             pltpu.VMEM((steps, seqs, width), F32),
             pltpu.VMEM((steps, 1, width), F32),
@@ -495,7 +570,7 @@
             pltpu.VMEM((segments, steps, block, padded), F32),
             pltpu.VMEM((steps, block, padded), F32),
             pltpu.VMEM((inner, steps, block, 128), F32),
-            dma,
+            dma((3,)),
             dma((6,)),
             dma,
             dma((inner * 3,)),
@@ -520,20 +595,20 @@
             collective_id=0, has_side_effects=True, vmem_limit_bytes=60 * 1024 * 1024
         ),
     )(*operands)
-    is_short = lax.axis_index("segment") % 2 == 0
-    shifted = jnp.concatenate([fir_by_tap[0], product], axis=0)[steps:]
-    fir_out = jnp.where(is_short, shifted, fir_by_tap[0])
-    decay = jnp.exp(-modal_rate[0])[None]
-    mode_values = modal_state[0]
-    for t in range(steps):
-        mode_values = decay * mode_values + (1.0 - decay) * product[t][:, None, :]
-    modal_out = jnp.where(is_short, modal_state[0], mode_values)
-    return (
-        packed[..., :vocab_local],
-        packed[..., padded],
-        jnp.transpose(fir_out, (1, 0, 2))[None],
-        modal_out[None],
-    )
+    logits, logprob, fir_out, modal_out = pl.pallas_call(
+        functools.partial(hand_out, vocab_local, padded),
+        out_shape=(
+            jax.ShapeDtypeStruct((steps, block, vocab_local), F32),
+            jax.ShapeDtypeStruct((steps, block), F32),
+            jax.ShapeDtypeStruct(fir_by_tap.shape, F32),
+            jax.ShapeDtypeStruct(modal_state.shape, F32),
+        ),
+        in_specs=[whole, in_hbm, in_hbm],
+        out_specs=(whole, whole, in_hbm, in_hbm),
+        scratch_shapes=[dma((2,))],
+        compiler_params=pltpu.CompilerParams(vmem_limit_bytes=60 * 1024 * 1024),
+    )(packed, fir_new, modal_new)
+    return (logits, logprob, jnp.transpose(fir_out, (0, 2, 1, 3)), modal_out)
 
 
 def solution(mesh):

time: 93.7 us -> 152 us (1.62)
  Pallas kernels: 86 us -> 151 us
  local copies, waits for them, and re-layouts: 3.64 us -> 0 us
  other arithmetic: 3.13 us -> 0 us
    pallas_call x0 -> x1, Pallas kernels: none -> 58 us  [per_device(): pl.pallas_call(functools.partial(hand_out, vocab_local, padded), out_shap...]
    pallas_call x1, Pallas kernels: 86 us -> 93.3 us  [per_device(): pl.pallas_call(functools.partial(kernel, pieces, inner, segments), out_sh...]
    slice x2 -> x0, local copies, waits for them, and re-layouts: 2.64 us -> none  [the longest x1 1.34 us: per_device(): packed[..., padded]]
    broadcast_in_dim x1 -> x0, other arithmetic: 1.9 us -> none  [per_device(): jnp.transpose(fir_out, (1, 0, 2))[None]]
where the time goes in v3:
time: 152 us
  Pallas kernels  151 us (99%)
    pallas_call x1, Pallas kernels, per_device(): pl.pallas_call(functools.partial(kernel, pieces, inner, segments), out_sh...  93.3 us
    pallas_call x1, Pallas kernels, per_device(): pl.pallas_call(functools.partial(hand_out, vocab_local, padded), out_shap...  58 us

profile of v3, /device:TPU:0, one launch (start us, length us, event | category | flops | bytes accessed | tf_op | source)
XLA Modules:
  0.0 152.0 jit_solution(6570223946516827218)
XLA Ops:
  0.6 93.3 %shard_map.147 = (f32[2,8,256]{2,1,0:T(8,128)}, f32[6,32,1024]{2,1,0:T(8,128)}, f32[32,8,1024]{2,1,0:T(8,128)}) custom-call(s32[3,32]{1,0:T(4,128)} %tokens_h.1, f32[1,4096]{1,0:T(1,128)} %norm_gain_h.1, f32[1,4096]{1,0:T(1,128)} %bitcast.6, f32[7,1,1024]{2,1,0:T(1,128)} %bitcast.5, f32[1,8,1024]{2,1,0:T(8,128)} %rate_h.1, f32[1,8,1024]{2,1,0:T(8,128)} %residue_h.1, ...), custom_call_target="tpu_custom_call" | custom-call | tf_op jit(solution)/shard_map/pallas_call | solution.py:538
  94.0 58.0 %shard_map.148 = (f32[2,8,128]{2,1,0:T(8,128)}, f32[2,8]{1,0:T(2,128)}, f32[1,6,32,1024]{3,2,1,0:T(8,128)}, f32[1,32,8,1024]{3,2,1,0:T(8,128)}) custom-call(f32[2,8,256]{2,1,0:T(8,128)} %get-tuple-element.11.packed, f32[6,32,1024]{2,1,0:T(8,128)} %get-tuple-element.12.fir_new, f32[32,8,1024]{2,1,0:T(8,128)} %get-tuple-element.13.modal_new), custom_call_target="tpu_custom_call" | custom-call | tf_op jit(solution)/shard_map/pallas_call | solution.py:598

commit v4 on v3

--- a/solution.py
+++ b/solution.py
@@ -77,8 +77,8 @@
         )
 
     emb_copy = pltpu.make_async_copy(embedding, emb_v, emb_sem)
-    fir_copy = pltpu.make_async_copy(fir_state.at[0], fir_v, state_sem)
-    modal_copy = pltpu.make_async_copy(modal_state.at[0], modal_v, state_sem)
+    fir_copy = pltpu.make_async_copy(fir_state.at[0], fir_v, state_sem.at[0])
+    modal_copy = pltpu.make_async_copy(modal_state.at[0], modal_v, state_sem.at[1])
     unembed_copy = pltpu.make_async_copy(unembed, unembed_v, unembed_sem)
     small = [
         pltpu.make_async_copy(source, target, small_sem.at[index])
@@ -131,26 +131,24 @@
 
     unembed_copy.start()
 
-    fir_whole = pltpu.make_async_copy(fir_state.at[0], fir_new, out_state_sem.at[0])
+    @pl.when(is_short)
+    def _():
+        modal_copy.start()
+
+    @pl.when(jnp.logical_not(is_short))
+    def _():
+        fir_copy.start()
+
+    fir_whole = pltpu.make_async_copy(fir_v, fir_new, out_state_sem.at[0])
     fir_shift = pltpu.make_async_copy(
-        fir_state.at[0, pl.ds(steps, depth - steps)],
+        fir_v.at[pl.ds(steps, depth - steps)],
         fir_new.at[pl.ds(0, depth - steps)],
         out_state_sem.at[0],
     )
     fir_latest = pltpu.make_async_copy(
         product_v, fir_new.at[pl.ds(depth - steps, steps)], out_state_sem.at[1]
     )
-    modal_whole = pltpu.make_async_copy(modal_state.at[0], modal_new, out_state_sem.at[2])
     modal_done = pltpu.make_async_copy(modal_v, modal_new, out_state_sem.at[2])
-
-    @pl.when(is_short)
-    def _():
-        fir_shift.start()
-        modal_whole.start()
-
-    @pl.when(jnp.logical_not(is_short))
-    def _():
-        fir_whole.start()
 
     small[0].wait()
 
@@ -308,6 +306,7 @@
 
     @pl.when(is_short)
     def _():
+        fir_shift.start()
         fir_latest.start()
 
     def a_copy(k):
@@ -365,8 +364,14 @@
             def _():
                 spread(f_copy, k)
 
+    @pl.when(is_short)
+    def _():
+        modal_copy.wait()
+
     @pl.when(jnp.logical_not(is_short))
     def _():
+        fir_copy.wait()
+        fir_whole.start()
         decay = jnp.exp(-rate[0])
 
         @pl.loop(0, seqs)
@@ -376,7 +381,7 @@
                 value = decay * value + (1.0 - decay) * product_v[t, pl.ds(b, 1), :]
             modal_v[b] = value
 
-        modal_done.start()
+    modal_done.start()
 
     unembed_copy.wait()
 
@@ -456,12 +461,12 @@
     def _():
         fir_shift.wait()
         fir_latest.wait()
-        modal_whole.wait()
 
     @pl.when(jnp.logical_not(is_short))
     def _():
         fir_whole.wait()
-        modal_done.wait()
+
+    modal_done.wait()
 
     @pl.loop(0, pieces)
     def _(k):
@@ -492,12 +497,22 @@
         e_copy(p).wait_send()
 
 
-def hand_out(vocab_local, padded, packed, fir_new, modal_new, logits, logprob, fir, modal, sems):
-    copies = [
-        pltpu.make_async_copy(fir_new, fir.at[0], sems.at[0]),
-        pltpu.make_async_copy(modal_new, modal.at[0], sems.at[1]),
+def hand_out(
+    vocab_local, padded, packed, fir_new, modal_new, logits, logprob, fir, modal,
+    fir_v, modal_v, in_sems, out_sems,
+):
+    parts = [(fir_new, fir_v, fir, i) for i in range(fir_v.shape[0])]
+    share = modal_v.shape[0] // 4
+    parts += [(modal_new, modal_v, modal, pl.ds(i * share, share)) for i in range(4)]
+    arriving = [
+        pltpu.make_async_copy(source.at[where], held.at[where], in_sems.at[i])
+        for i, (source, held, _, where) in enumerate(parts)
     ]
-    for copy in copies:
+    leaving = [
+        pltpu.make_async_copy(held.at[where], target.at[0, where], out_sems.at[i])
+        for i, (_, held, target, where) in enumerate(parts)
+    ]
+    for copy in arriving:
         copy.start()
     steps, block = logprob.shape
     down = lax.broadcasted_iota(jnp.int32, (block, block), 0)
@@ -508,7 +523,10 @@
         logprob[t:t + 1, :] = jnp.sum(
             jnp.where(down == across, spread_out, 0.0), axis=0, keepdims=True
         )
-    for copy in copies:
+    for before, after in zip(arriving, leaving):
+        before.wait()
+        after.start()
+    for copy in leaving:
         copy.wait()
 
 
@@ -575,7 +593,7 @@
             dma,
             dma((inner * 3,)),
             dma((inner * pieces,)),
-            dma,
+            dma((2,)),
             dma,
             dma((inner * pieces,)),
             dma((inner * pieces,)),
@@ -605,7 +623,12 @@
         ),
         in_specs=[whole, in_hbm, in_hbm],
         out_specs=(whole, whole, in_hbm, in_hbm),
-        scratch_shapes=[dma((2,))],
+        scratch_shapes=[
+            pltpu.VMEM(fir_new.shape, F32),
+            pltpu.VMEM(modal_new.shape, F32),
+            dma((fir_new.shape[0] + 4,)),
+            dma((fir_new.shape[0] + 4,)),
+        ],
         compiler_params=pltpu.CompilerParams(vmem_limit_bytes=60 * 1024 * 1024),
     )(packed, fir_new, modal_new)
     return (logits, logprob, jnp.transpose(fir_out, (0, 2, 1, 3)), modal_out)

time: 152 us -> 98 us (0.64)
  Pallas kernels: 151 us -> 97.1 us
    pallas_call x1, Pallas kernels: 58 us -> 3.74 us  [per_device(): pl.pallas_call(functools.partial(hand_out, vocab_local, padded), out_shap...]
where the time goes in v4:
time: 98 us; the launch traced here: 97.7 us
  Pallas kernels  97.1 us (99%)
    pallas_call x1, Pallas kernels, per_device(): pl.pallas_call(functools.partial(kernel, pieces, inner, segments), out_sh...  93.4 us
    pallas_call x1, Pallas kernels, per_device(): pl.pallas_call(functools.partial(hand_out, vocab_local, padded), out_shap...  3.74 us

profile of v4, /device:TPU:0, one launch (start us, length us, event | category | flops | bytes accessed | tf_op | source)
XLA Modules:
  0.0 97.7 jit_solution(11643712544184700900)
XLA Ops:
  0.6 93.4 %shard_map.147 = (f32[2,8,256]{2,1,0:T(8,128)}, f32[6,32,1024]{2,1,0:T(8,128)}, f32[32,8,1024]{2,1,0:T(8,128)}) custom-call(s32[3,32]{1,0:T(4,128)} %tokens_h.1, f32[1,4096]{1,0:T(1,128)} %norm_gain_h.1, f32[1,4096]{1,0:T(1,128)} %bitcast.6, f32[7,1,1024]{2,1,0:T(1,128)} %bitcast.5, f32[1,8,1024]{2,1,0:T(8,128)} %rate_h.1, f32[1,8,1024]{2,1,0:T(8,128)} %residue_h.1, ...), custom_call_target="tpu_custom_call" | custom-call | tf_op jit(solution)/shard_map/pallas_call | solution.py:556
  94.0 3.7 %shard_map.148 = (f32[2,8,128]{2,1,0:T(8,128)}, f32[2,8]{1,0:T(2,128)}, f32[1,6,32,1024]{3,2,1,0:T(8,128)}, f32[1,32,8,1024]{3,2,1,0:T(8,128)}) custom-call(f32[2,8,256]{2,1,0:T(8,128)} %get-tuple-element.11.packed, f32[6,32,1024]{2,1,0:T(8,128)} %get-tuple-element.12.fir_new, f32[32,8,1024]{2,1,0:T(8,128)} %get-tuple-element.13.modal_new), custom_call_target="tpu_custom_call" | custom-call | tf_op jit(solution)/shard_map/pallas_call | solution.py:616

commit v5 on v4

--- a/solution.py
+++ b/solution.py
@@ -119,11 +119,9 @@
     def _():
         modal_copy.start()
 
-    for dx, dc in (
-        [(0, 0), (0, 1)] + [(dx, 0) for dx in range(1, chips)] + [(dx, 1) for dx in range(1, chips)]
-    ):
+    for t in range(inner):
         for j in range(3):
-            in_copy(member(dx, dc), j).start()
+            in_copy(member(t % chips, t // chips), j).start()
 
     @pl.loop(0, pieces * inner)
     def _(t):
@@ -251,34 +249,21 @@
     def block_of(buf, q):
         return jnp.concatenate([buf[q * pieces + k] for k in range(pieces)], axis=1)
 
-    @pl.loop(0, pieces)
-    def _(k):
-        @pl.when(seg > 0)
-        def _():
+    @pl.when(seg > 0)
+    def _():
+        for k in range(pieces):
             arrival(xbuf.at[me * pieces + k], x_recv.at[me * pieces + k])
             spread(x_copy, k)
 
-        @pl.when(k == 0)
-        def _():
-            for j in range(3):
-                in_copy(me, j).wait()
-
-        offset = pl.multiple_of(me * width + k * sub, sub)
-        scaled = take(xbuf[me * pieces + k], norm_gain[:, pl.ds(offset, sub)])
-        depth_rows = pl.ds(pl.multiple_of(k * sub, sub), sub)
-        for j in range(3):
-            acc[j] += jnp.dot(scaled, in_v[me, j, depth_rows, :], preferred_element_type=F32)
-
-    @pl.loop(1, inner)
+    @pl.loop(0, inner)
     def _(t):
-        q = member(jnp.where(t == 1, 0, jnp.where(t <= chips, t - 1, t - chips)),
-                   jnp.where((t == 1) | (t > chips), 1, 0))
-
-        @pl.when(t == 2)
+        q = member(t % chips, t // chips)
+
+        @pl.when(t == 1)
         def _():
             pass_on(xbuf, x_send, x_recv)
 
-        @pl.when((t == 1) | (t > chips))
+        @pl.when(t >= chips)
         def _():
             for k in range(pieces):
                 arrival(xbuf.at[q * pieces + k], x_recv.at[q * pieces + k])
@@ -328,41 +313,46 @@
         out_copy(q, k).wait()
         return jnp.dot(gated[...], out_v[q * pieces + k], preferred_element_type=F32)
 
-    for step in range(pieces + 2):
-        k = step
-        if k < pieces:
-            for x in range(chips):
-                abuf[k, x] = mix(x * 2 + (core + 1) % 2, k).astype(BF16)
-            a_copy(k).start()
-        k = step - 1
-        if 0 <= k < pieces:
-            arrival(arbuf.at[k], a_recv.at[k])
-            for dx in range(chips - 1, 0, -1):
-                total = mixed[k, dx] + arbuf[k, (chip + dx) % chips].astype(F32)
-                bbuf[dx * pieces + k] = total.astype(BF16)
-                b_copy(k, dx).start()
-            total = mixed[k, 0] + arbuf[k, chip].astype(F32)
-            mixed[k, 0] = total + xbuf[me * pieces + k].astype(F32)
-        k = step
-        if k < pieces:
-            for dx in range(chips - 1, -1, -1):
-                mixed[k, dx] = mix(member(dx, 0), k)
-        k = step - 2
-        if 0 <= k < pieces:
-            total = mixed[k, 0]
-            for dx in range(1, chips):
-                source = (chip + dx) % chips * pieces + k
-                arrival(brbuf.at[source], b_recv.at[source])
-                total = total + brbuf[source].astype(F32)
-            zbuf[k] = total.astype(BF16)
-
-            @pl.when(seg < last)
-            def _():
-                z_copy(k).start()
-
-            @pl.when(seg == last)
-            def _():
-                spread(f_copy, k)
+    @pl.loop(0, pieces)
+    def _(k):
+        for x in range(chips):
+            abuf[k, x] = mix(x * 2 + (core + 1) % 2, k).astype(BF16)
+        a_copy(k).start()
+
+    @pl.loop(0, pieces)
+    def _(k):
+        for dx in range(1, chips):
+            mixed[k, dx] = mix(member(dx, 0), k)
+
+    @pl.loop(0, pieces)
+    def _(k):
+        arrival(arbuf.at[k], a_recv.at[k])
+        for dx in range(chips - 1, 0, -1):
+            total = mixed[k, dx] + arbuf[k, (chip + dx) % chips].astype(F32)
+            bbuf[dx * pieces + k] = total.astype(BF16)
+            b_copy(k, dx).start()
+
+    @pl.loop(0, pieces)
+    def _(k):
+        total = mix(me, k) + arbuf[k, chip].astype(F32)
+        mixed[k, 0] = total + xbuf[me * pieces + k].astype(F32)
+
+    @pl.loop(0, pieces)
+    def _(k):
+        total = mixed[k, 0]
+        for dx in range(1, chips):
+            source = (chip + dx) % chips * pieces + k
+            arrival(brbuf.at[source], b_recv.at[source])
+            total = total + brbuf[source].astype(F32)
+        zbuf[k] = total.astype(BF16)
+
+        @pl.when(seg < last)
+        def _():
+            z_copy(k).start()
+
+        @pl.when(seg == last)
+        def _():
+            spread(f_copy, k)
 
     @pl.when(is_short)
     def _():

time: 98 us -> 96.4 us (0.984)
  Pallas kernels: 97.1 us -> 95.6 us
    pallas_call x1, Pallas kernels: 93.4 us -> 91.8 us  [per_device(): pl.pallas_call(functools.partial(kernel, pieces, inner, segments), out_sh...]
where the time goes in v5:
time: 96.4 us; the launch traced here: 96.2 us
  Pallas kernels  95.6 us (99%)
    pallas_call x1, Pallas kernels, per_device(): pl.pallas_call(functools.partial(kernel, pieces, inner, segments), out_sh...  91.8 us
    pallas_call x1, Pallas kernels, per_device(): pl.pallas_call(functools.partial(hand_out, vocab_local, padded), out_shap...  3.74 us

profile of v5, /device:TPU:0, one launch (start us, length us, event | category | flops | bytes accessed | tf_op | source)
XLA Modules:
  0.0 96.2 jit_solution(4452476044086153906)
XLA Ops:
  0.6 91.8 %shard_map.147 = (f32[2,8,256]{2,1,0:T(8,128)}, f32[6,32,1024]{2,1,0:T(8,128)}, f32[32,8,1024]{2,1,0:T(8,128)}) custom-call(s32[3,32]{1,0:T(4,128)} %tokens_h.1, f32[1,4096]{1,0:T(1,128)} %norm_gain_h.1, f32[1,4096]{1,0:T(1,128)} %bitcast.6, f32[7,1,1024]{2,1,0:T(1,128)} %bitcast.5, f32[1,8,1024]{2,1,0:T(8,128)} %rate_h.1, f32[1,8,1024]{2,1,0:T(8,128)} %residue_h.1, ...), custom_call_target="tpu_custom_call" | custom-call | tf_op jit(solution)/shard_map/pallas_call | solution.py:546
  92.5 3.7 %shard_map.148 = (f32[2,8,128]{2,1,0:T(8,128)}, f32[2,8]{1,0:T(2,128)}, f32[1,6,32,1024]{3,2,1,0:T(8,128)}, f32[1,32,8,1024]{3,2,1,0:T(8,128)}) custom-call(f32[2,8,256]{2,1,0:T(8,128)} %get-tuple-element.11.packed, f32[6,32,1024]{2,1,0:T(8,128)} %get-tuple-element.12.fir_new, f32[32,8,1024]{2,1,0:T(8,128)} %get-tuple-element.13.modal_new), custom_call_target="tpu_custom_call" | custom-call | tf_op jit(solution)/shard_map/pallas_call | solution.py:606

commit v6 on v5

--- a/solution.py
+++ b/solution.py
@@ -315,31 +315,29 @@
 
     @pl.loop(0, pieces)
     def _(k):
-        for x in range(chips):
+        @pl.loop(0, chips)
+        def _(x):
             abuf[k, x] = mix(x * 2 + (core + 1) % 2, k).astype(BF16)
+
         a_copy(k).start()
 
     @pl.loop(0, pieces)
     def _(k):
-        for dx in range(1, chips):
-            mixed[k, dx] = mix(member(dx, 0), k)
+        for dx in range(chips - 1, -1, -1):
+            mixed[dx] = mix(member(dx, 0), k)
+        arrival(arbuf.at[k], a_recv.at[k])
+        for dx in range(chips - 1, 0, -1):
+            total = mixed[dx] + arbuf[k, (chip + dx) % chips].astype(F32)
+            bbuf[dx * pieces + k] = total.astype(BF16)
+            b_copy(k, dx).start()
+        total = mixed[0] + arbuf[k, chip].astype(F32)
+        acc[0, :, pl.ds(pl.multiple_of(k * sub, sub), sub)] = (
+            total + xbuf[me * pieces + k].astype(F32)
+        )
 
     @pl.loop(0, pieces)
     def _(k):
-        arrival(arbuf.at[k], a_recv.at[k])
-        for dx in range(chips - 1, 0, -1):
-            total = mixed[k, dx] + arbuf[k, (chip + dx) % chips].astype(F32)
-            bbuf[dx * pieces + k] = total.astype(BF16)
-            b_copy(k, dx).start()
-
-    @pl.loop(0, pieces)
-    def _(k):
-        total = mix(me, k) + arbuf[k, chip].astype(F32)
-        mixed[k, 0] = total + xbuf[me * pieces + k].astype(F32)
-
-    @pl.loop(0, pieces)
-    def _(k):
-        total = mixed[k, 0]
+        total = acc[0, :, pl.ds(pl.multiple_of(k * sub, sub), sub)]
         for dx in range(1, chips):
             source = (chip + dx) % chips * pieces + k
             arrival(brbuf.at[source], b_recv.at[source])
@@ -354,24 +352,25 @@
         def _():
             spread(f_copy, k)
 
-    @pl.when(is_short)
-    def _():
-        modal_copy.wait()
-
-    @pl.when(jnp.logical_not(is_short))
-    def _():
-        fir_copy.wait()
-        fir_whole.start()
-        decay = jnp.exp(-rate[0])
-
-        @pl.loop(0, seqs)
-        def _(b):
-            value = modal_v[b]
-            for t in range(steps):
-                value = decay * value + (1.0 - decay) * product_v[t, pl.ds(b, 1), :]
-            modal_v[b] = value
-
-    modal_done.start()
+    def finish_states():
+        @pl.when(is_short)
+        def _():
+            modal_copy.wait()
+
+        @pl.when(jnp.logical_not(is_short))
+        def _():
+            fir_copy.wait()
+            fir_whole.start()
+            decay = jnp.exp(-rate[0])
+
+            @pl.loop(0, seqs)
+            def _(b):
+                value = modal_v[b]
+                for t in range(steps):
+                    value = decay * value + (1.0 - decay) * product_v[t, pl.ds(b, 1), :]
+                modal_v[b] = value
+
+        modal_done.start()
 
     unembed_copy.wait()
 
@@ -418,6 +417,7 @@
 
     @pl.when(seg < last)
     def _():
+        finish_states()
         arrival(lbuf, l_recv)
 
     def e_copy(p):
@@ -438,6 +438,11 @@
         ebuf[me, t] = jnp.where(lanes == 0, exp_sum, target_part)
     for p in range(inner - 1, 0, -1):
         e_copy(p).start()
+
+    @pl.when(seg == last)
+    def _():
+        finish_states()
+
     sums = ebuf[me]
     for p in range(1, inner):
         q = member(p // 2, p % 2)
@@ -489,11 +494,15 @@
 
 def hand_out(
     vocab_local, padded, packed, fir_new, modal_new, logits, logprob, fir, modal,
-    fir_v, modal_v, in_sems, out_sems,
+    packed_v, logits_v, logprob_v, fir_v, modal_v, in_sems, out_sems,
 ):
-    parts = [(fir_new, fir_v, fir, i) for i in range(fir_v.shape[0])]
-    share = modal_v.shape[0] // 4
-    parts += [(modal_new, modal_v, modal, pl.ds(i * share, share)) for i in range(4)]
+    half = fir_v.shape[0] // 2
+    share = modal_v.shape[0] // 2
+    parts = [(fir_new, fir_v, fir, pl.ds(i * half, half)) for i in range(2)]
+    parts += [(modal_new, modal_v, modal, pl.ds(i * share, share)) for i in range(2)]
+    packed_copy = pltpu.make_async_copy(packed, packed_v, in_sems.at[4])
+    logits_copy = pltpu.make_async_copy(logits_v, logits, out_sems.at[4])
+    logprob_copy = pltpu.make_async_copy(logprob_v, logprob, out_sems.at[5])
     arriving = [
         pltpu.make_async_copy(source.at[where], held.at[where], in_sems.at[i])
         for i, (source, held, _, where) in enumerate(parts)
@@ -502,22 +511,28 @@
         pltpu.make_async_copy(held.at[where], target.at[0, where], out_sems.at[i])
         for i, (_, held, target, where) in enumerate(parts)
     ]
+    packed_copy.start()
     for copy in arriving:
         copy.start()
+    packed_copy.wait()
     steps, block = logprob.shape
     down = lax.broadcasted_iota(jnp.int32, (block, block), 0)
     across = lax.broadcasted_iota(jnp.int32, (block, block), 1)
     for t in range(steps):
-        logits[t] = packed[t, :, :vocab_local]
-        spread_out = packed[t, :, padded:padded + block]
-        logprob[t:t + 1, :] = jnp.sum(
+        logits_v[t] = packed_v[t, :, :vocab_local]
+        spread_out = packed_v[t, :, padded:padded + block]
+        logprob_v[t:t + 1, :] = jnp.sum(
             jnp.where(down == across, spread_out, 0.0), axis=0, keepdims=True
         )
+    logits_copy.start()
+    logprob_copy.start()
     for before, after in zip(arriving, leaving):
         before.wait()
         after.start()
     for copy in leaving:
         copy.wait()
+    logits_copy.wait()
+    logprob_copy.wait()
 
 
 def per_device(
@@ -569,7 +584,7 @@
             pltpu.VMEM((chips * pieces, rows, sub), BF16),
             pltpu.VMEM((pieces, rows, sub), BF16),
             pltpu.VMEM((3, rows, width), F32),
-            pltpu.VMEM((pieces, chips, rows, sub), F32),
+            pltpu.VMEM((chips, rows, sub), F32),
             pltpu.VMEM((rows, 128), F32),
             pltpu.VMEM((steps, seqs, width), F32),
             pltpu.VMEM((steps, 1, width), F32),
@@ -611,13 +626,16 @@
             jax.ShapeDtypeStruct(fir_by_tap.shape, F32),
             jax.ShapeDtypeStruct(modal_state.shape, F32),
         ),
-        in_specs=[whole, in_hbm, in_hbm],
-        out_specs=(whole, whole, in_hbm, in_hbm),
+        in_specs=[in_hbm] * 3,
+        out_specs=(in_hbm,) * 4,
         scratch_shapes=[
+            pltpu.VMEM(packed.shape, F32),
+            pltpu.VMEM((steps, block, vocab_local), F32),
+            pltpu.VMEM((steps, block), F32),
             pltpu.VMEM(fir_new.shape, F32),
             pltpu.VMEM(modal_new.shape, F32),
-            dma((fir_new.shape[0] + 4,)),
-            dma((fir_new.shape[0] + 4,)),
+            dma((5,)),
+            dma((6,)),
         ],
         compiler_params=pltpu.CompilerParams(vmem_limit_bytes=60 * 1024 * 1024),
     )(packed, fir_new, modal_new)

time: 96.4 us -> 94.2 us (0.977)
  Pallas kernels: 95.6 us -> 93.3 us
    pallas_call x1, Pallas kernels: 3.74 us -> 2.36 us  [per_device(): pl.pallas_call(functools.partial(hand_out, vocab_local, padded), out_shap...]
where the time goes in v6:
time: 94.2 us; the launch traced here: 93.9 us
  Pallas kernels  93.3 us (99%)
    pallas_call x1, Pallas kernels, per_device(): pl.pallas_call(functools.partial(kernel, pieces, inner, segments), out_sh...  90.9 us
    pallas_call x1, Pallas kernels, per_device(): pl.pallas_call(functools.partial(hand_out, vocab_local, padded), out_shap...  2.36 us

profile of v6, /device:TPU:0, one launch (start us, length us, event | category | flops | bytes accessed | tf_op | source)
XLA Modules:
  0.0 93.9 jit_solution(4470268653337541127)
XLA Ops:
  0.6 90.9 %shard_map.147 = (f32[2,8,256]{2,1,0:T(8,128)}, f32[6,32,1024]{2,1,0:T(8,128)}, f32[32,8,1024]{2,1,0:T(8,128)}) custom-call(s32[3,32]{1,0:T(4,128)} %tokens_h.1, f32[1,4096]{1,0:T(1,128)} %norm_gain_h.1, f32[1,4096]{1,0:T(1,128)} %bitcast.6, f32[7,1,1024]{2,1,0:T(1,128)} %bitcast.5, f32[1,8,1024]{2,1,0:T(8,128)} %rate_h.1, f32[1,8,1024]{2,1,0:T(8,128)} %residue_h.1, ...), custom_call_target="tpu_custom_call" | custom-call | tf_op jit(solution)/shard_map/pallas_call | solution.py:561
  91.5 2.4 %shard_map.148 = (f32[2,8,128]{2,1,0:T(8,128)}, f32[2,8]{1,0:T(2,128)}, f32[1,6,32,1024]{3,2,1,0:T(8,128)}, f32[1,32,8,1024]{3,2,1,0:T(8,128)}) custom-call(f32[2,8,256]{2,1,0:T(8,128)} %get-tuple-element.11.packed, f32[6,32,1024]{2,1,0:T(8,128)} %get-tuple-element.12.fir_new, f32[32,8,1024]{2,1,0:T(8,128)} %get-tuple-element.13.modal_new), custom_call_target="tpu_custom_call" | custom-call | tf_op jit(solution)/shard_map/pallas_call | solution.py:621

commit v7 on v6

--- a/solution.py
+++ b/solution.py
@@ -222,6 +222,8 @@
 
     @pl.when(jnp.logical_not(is_short))
     def _():
+        fir_copy.wait()
+        fir_whole.start()
         decay = jnp.exp(-rate[0])
         weight = residue[0] * (1.0 - decay)
         for t in range(steps):
@@ -289,11 +291,6 @@
                 filtered = filtered + coefs[t - u, :, cols] * products[u]
             gated[part, cols] = (acc[0, part, cols] * scale_t * filtered).astype(BF16)
 
-    @pl.when(is_short)
-    def _():
-        fir_shift.start()
-        fir_latest.start()
-
     def a_copy(k):
         return remote(abuf.at[k], arbuf.at[k], a_send.at[k], a_recv.at[k], {"inner": sibling})
 
@@ -355,12 +352,12 @@
     def finish_states():
         @pl.when(is_short)
         def _():
+            fir_shift.start()
+            fir_latest.start()
             modal_copy.wait()
 
         @pl.when(jnp.logical_not(is_short))
         def _():
-            fir_copy.wait()
-            fir_whole.start()
             decay = jnp.exp(-rate[0])
 
             @pl.loop(0, seqs)

time: 94.2 us -> 94.2 us (level)
  no operation moved by 1% of the time
where the time goes in v7:
time: 94.2 us; the launch traced here: 93.9 us
  Pallas kernels  93.3 us (99%)
    pallas_call x1, Pallas kernels, per_device(): pl.pallas_call(functools.partial(kernel, pieces, inner, segments), out_sh...  90.9 us
    pallas_call x1, Pallas kernels, per_device(): pl.pallas_call(functools.partial(hand_out, vocab_local, padded), out_shap...  2.36 us

profile of v7, /device:TPU:0, one launch (start us, length us, event | category | flops | bytes accessed | tf_op | source)
XLA Modules:
  0.0 93.9 jit_solution(5649788275353235936)
XLA Ops:
  0.6 90.9 %shard_map.147 = (f32[2,8,256]{2,1,0:T(8,128)}, f32[6,32,1024]{2,1,0:T(8,128)}, f32[32,8,1024]{2,1,0:T(8,128)}) custom-call(s32[3,32]{1,0:T(4,128)} %tokens_h.1, f32[1,4096]{1,0:T(1,128)} %norm_gain_h.1, f32[1,4096]{1,0:T(1,128)} %bitcast.6, f32[7,1,1024]{2,1,0:T(1,128)} %bitcast.5, f32[1,8,1024]{2,1,0:T(8,128)} %rate_h.1, f32[1,8,1024]{2,1,0:T(8,128)} %residue_h.1, ...), custom_call_target="tpu_custom_call" | custom-call | tf_op jit(solution)/shard_map/pallas_call | solution.py:558
  91.5 2.4 %shard_map.148 = (f32[2,8,128]{2,1,0:T(8,128)}, f32[2,8]{1,0:T(2,128)}, f32[1,6,32,1024]{3,2,1,0:T(8,128)}, f32[1,32,8,1024]{3,2,1,0:T(8,128)}) custom-call(f32[2,8,256]{2,1,0:T(8,128)} %get-tuple-element.11.packed, f32[6,32,1024]{2,1,0:T(8,128)} %get-tuple-element.12.fir_new, f32[32,8,1024]{2,1,0:T(8,128)} %get-tuple-element.13.modal_new), custom_call_target="tpu_custom_call" | custom-call | tf_op jit(solution)/shard_map/pallas_call | solution.py:618
